TPU v7x, 32 devices: a whole 2x2x4 slice. The times are simulated.
32 devices in a mesh: wave: 2 (over x), region: 16 (over z, y, core).
Axes of the slice: x: 2, y: 2, z: 4, core: 2. Of those that a mesh axis runs over, the one named last changes fastest.
Arguments:
- object_field: float32 [2, 8192, 1024], P(None, 'region'), may hold values from -5 to 5
- probes: float32 [2, 2, 256, 256], P('wave'), may hold values from -5 to 5
- patterns: bfloat16 [2, 256, 256, 256], P('wave', 'region'), may hold values from 0 to 2
- offsets: int32 [256, 2], P('region'), may hold values from 0 to 768, as said below
- counts: int32 [16], P('region'), may hold values from 1 to 16, as said below
Outputs:
- object_grad: float32 [2, 8192, 1024], P(None, 'region', 'wave')
- probe_grad: float32 [2, 2, 256, 256], P('wave')
Inputs may be any that keep to these rules, and one draw needn't show every extreme that they name: Offsets are whole cells: row offsets below 512, column offsets at most 768. `counts`: some tile uses all slots and some tile uses one.
All inputs are finite; a program needn't handle non-finite values.
Results may differ from a plain program's by a relative error of at most 0.0052.
Values sent between devices are 32-bit elements; how exact they have to be, the bound alone decides.
A program may use at most 128 MiB of HBM per device.

v0:
```python
import math

import jax
import jax.numpy as jnp
from jax import lax
from jax.sharding import PartitionSpec as P


def from_behind(block, axis, distance):
    devices = range(lax.axis_size(axis))
    route = [(i - distance, i) for i in devices if i - distance in devices]
    return lax.ppermute(block, axis, route)


def make_tables(patch_side):
    index = jnp.arange(patch_side, dtype=jnp.int32)
    phase_int = index[:, None] * index[None, :] % patch_side
    phase = phase_int.astype(jnp.float32) * (2.0 * math.pi / patch_side)
    scale = 1.0 / math.sqrt(patch_side)
    return (
        (jnp.cos(phase) * scale).astype(jnp.bfloat16),
        (jnp.sin(phase) * scale).astype(jnp.bfloat16),
    )


def apply_left(table, field_part):
    return jnp.einsum("kn,bnm->bkm", table, field_part, preferred_element_type=jnp.float32)


def apply_right(field_part, table):
    return jnp.einsum("bkn,nm->bkm", field_part, table, preferred_element_type=jnp.float32)


def on_device(object_field, probes, patterns, offsets, counts):
    tile_rows = object_field.shape[1]
    width_cols = object_field.shape[2]
    patch_side = probes.shape[-1]
    slot_total = offsets.shape[0]
    top_rows = object_field[:, :patch_side, :]
    rim_rows = from_behind(top_rows, "region", -1)
    extended = jnp.concatenate([object_field, rim_rows], axis=1)
    zero_at = jnp.zeros((), jnp.int32)

    def extract(row_at, col_at):
        return lax.dynamic_slice(extended, (zero_at, row_at, col_at), (2, patch_side, patch_side))

    patches = jax.vmap(extract)(offsets[:, 0], offsets[:, 1])
    cos_table, sin_table = make_tables(patch_side)
    probe_re = probes[0, 0]
    probe_im = probes[0, 1]
    wave_re = (probe_re * patches[:, 0] - probe_im * patches[:, 1]).astype(jnp.bfloat16)
    wave_im = (probe_re * patches[:, 1] + probe_im * patches[:, 0]).astype(jnp.bfloat16)
    half_re = (apply_left(cos_table, wave_re) + apply_left(sin_table, wave_im)).astype(jnp.bfloat16)
    half_im = (apply_left(cos_table, wave_im) - apply_left(sin_table, wave_re)).astype(jnp.bfloat16)
    far_re = apply_right(half_re, cos_table) + apply_right(half_im, sin_table)
    far_im = apply_right(half_im, cos_table) - apply_right(half_re, sin_table)
    excess = far_re * far_re + far_im * far_im - patterns[0].astype(jnp.float32)
    back_re = (excess * far_re).astype(jnp.bfloat16)
    back_im = (excess * far_im).astype(jnp.bfloat16)
    inner_re = (apply_left(cos_table, back_re) - apply_left(sin_table, back_im)).astype(
        jnp.bfloat16
    )
    inner_im = (apply_left(cos_table, back_im) + apply_left(sin_table, back_re)).astype(
        jnp.bfloat16
    )
    chi_re = apply_right(inner_re, cos_table) - apply_right(inner_im, sin_table)
    chi_im = apply_right(inner_im, cos_table) + apply_right(inner_re, sin_table)
    in_use = (jnp.arange(slot_total, dtype=jnp.int32) < counts[0]).astype(jnp.float32)[
        :, None, None
    ]
    obj_terms = jnp.stack(
        [
            (probe_re * chi_re + probe_im * chi_im) * in_use,
            (probe_re * chi_im - probe_im * chi_re) * in_use,
        ],
        axis=1,
    )
    prb_re = jnp.sum((patches[:, 0] * chi_re + patches[:, 1] * chi_im) * in_use, axis=0)
    prb_im = jnp.sum((patches[:, 0] * chi_im - patches[:, 1] * chi_re) * in_use, axis=0)
    probe_total = lax.psum(jnp.stack([prb_re, prb_im]), "region")

    def accumulate(slot, grad_ext):
        row_at = offsets[slot, 0]
        col_at = offsets[slot, 1]
        current = lax.dynamic_slice(
            grad_ext, (zero_at, row_at, col_at), (2, patch_side, patch_side)
        )
        return lax.dynamic_update_slice(
            grad_ext, current + obj_terms[slot], (zero_at, row_at, col_at)
        )

    grad_ext = lax.fori_loop(
        0, slot_total, accumulate, jnp.zeros((2, tile_rows + patch_side, width_cols), jnp.float32)
    )
    arrived = from_behind(grad_ext[:, tile_rows:, :], "region", 1)
    tile_grad = grad_ext[:, :tile_rows, :] + jnp.pad(
        arrived, ((0, 0), (0, tile_rows - patch_side), (0, 0))
    )
    object_out = lax.psum_scatter(tile_grad, "wave", scatter_dimension=2, tiled=True)
    return (object_out, probe_total[None])


def solution(mesh):
    in_specs = (
        P(None, "region", None),
        P("wave", None, None, None),
        P("wave", "region", None, None),
        P("region", None),
        P("region"),
    )
    out_specs = (P(None, "region", "wave"), P("wave", None, None, None))
    return jax.shard_map(
        on_device, mesh=mesh, in_specs=in_specs, out_specs=out_specs, check_vma=False
    )
```

profile of v0, /device:TPU:0, one launch (start us, length us, event | category | flops | bytes accessed | tf_op | source)
XLA Modules:
  0.0 465.4 jit_solution(2377173944889016389)
XLA Ops:
  8.1 1.8 slice.34
  11.9 4.1 collective-permute-done
  16.0 6.7 %pad_maximum_fusion.1 = f32[2,768,1024]{2,1,0:T(8,128)} fusion(f32[2,256,1024]{2,1,0:T(8,128)} %collective-permute-done, f32[2,512,1024]{2,1,0:T(8,128)} %param.7), kind=kLoop, calls=%fused_computation.6 | loop fusion | flops 1572864 | bytes 12582912 | tf_op jit(solution)/shard_map/concatenate | solution.py:41
  22.7 63.8 %while.15 = (s32[]{:T(128)}, f32[2,768,1024]{2,1,0:T(8,128)}, s32[16,3]{0,1:T(4,128)S(1)}, f32[16,2,256,256]{3,2,0,1:T(8,128)}, s32[]{:T(128)}) while((s32[]{:T(128)}, f32[2,768,1024]{2,1,0:T(8,128)}, s32[16,3]{0,1:T(4,128)S(1)}, f32[16,2,256,256]{3,2,0,1:T(8,128)}, s32[]{:T(128)}) %tuple.58), condition=%wide.while_cond, body=%wide.while_body.sunk | while | flops 2 | bytes 1050217 | solution.py:45
  23.3 3.3 bitcast_dynamic-update-slice_fusion.2
  27.3 3.3 bitcast_dynamic-update-slice_fusion.2
  31.3 3.3 bitcast_dynamic-update-slice_fusion.2
  35.2 3.4 bitcast_dynamic-update-slice_fusion.2
  39.2 3.4 bitcast_dynamic-update-slice_fusion.2
  43.2 3.4 bitcast_dynamic-update-slice_fusion.2
  47.2 3.4 bitcast_dynamic-update-slice_fusion.2
  51.2 3.4 bitcast_dynamic-update-slice_fusion.2
  55.2 3.3 bitcast_dynamic-update-slice_fusion.2
  59.2 3.4 bitcast_dynamic-update-slice_fusion.2
  63.2 3.4 bitcast_dynamic-update-slice_fusion.2
  67.2 3.3 bitcast_dynamic-update-slice_fusion.2
  71.1 3.3 bitcast_dynamic-update-slice_fusion.2
  75.1 3.3 bitcast_dynamic-update-slice_fusion.2
  79.1 3.4 bitcast_dynamic-update-slice_fusion.2
  83.1 3.4 bitcast_dynamic-update-slice_fusion.2
  86.5 4.7 %fusion.3 = (bf16[16,256,256]{2,1,0:T(8,128)(2,1)S(1)}, bf16[16,256,256]{2,1,0:T(8,128)(2,1)S(1)}) fusion(f32[16,2,256,256]{3,2,0,1:T(8,128)} %get-tuple-element.89, f32[256,256]{1,0:T(8,128)S(1)} %get-tuple-element.125, f32[256,256]{1,0:T(8,128)S(1)} %get-tuple-element.124), kind=kLoop, calls=%fused_computation.15 | loop fusion | flops 8388608 | bytes 13107200 | tf_op jit(solution)/shard_map/convert_element_type | solution.py:52
  91.2 1.7 fusion.45
  92.8 1.7 fusion.48
  94.5 1.7 subtract_convert_fusion.1
  96.2 1.7 add_convert_fusion.1
  97.9 1.7 fusion.20
  99.6 1.7 fusion.16
  101.3 1.9 convolution_add_fusion.1
  103.2 2.9 multiply_convert_fusion
  106.1 1.7 fusion.42
  107.7 1.7 fusion.39
  109.4 1.7 subtract_convert_fusion
  111.1 1.7 add_convert_fusion
  112.8 1.7 fusion.10
  114.5 1.7 fusion.14
  116.2 1.7 convolution_add_fusion
  118.5 6.6 %fusion.6 = (f32[256,256]{1,0:T(8,128)}, f32[256,256]{1,0:T(8,128)}, f32[16,1,256,256]{3,2,0,1:T(8,128)S(1)}, f32[16,1,256,256]{3,2,0,1:T(8,128)S(1)}) fusion(f32[16,256,256]{2,1,0:T(8,128)S(1)} %convolution_add_fusion, f32[16,2,256,256]{3,2,0,1:T(8,128)S(1)} %bitcast.137, f32[16]{0:T(128)S(1)} %compare_convert_fusion, f32[256,256]{1,0:T(8,128)} %copy-done.2, ...), kind=kOutput, calls=%fused_computation.18 | convolution fusion | flops 557711360 | bytes 28311616 | tf_op jit(solution)/shard_map/bkn,nm->bkm/dot_general | solution.py:31
  125.1 4.1 pad_maximum_fusion
  129.2 3.5 broadcast_in_dim.4
  132.7 198.9 %while.14 = (s32[]{:T(128)}, f32[2,768,1024]{2,1,0:T(8,128)}, s32[16,2]{0,1:T(2,128)S(1)}, f32[16,2,256,256]{3,2,0,1:T(8,128)}, s32[]{:T(128)}, /*index=5*/s32[]{:T(128)}, s32[]{:T(128)}, s32[]{:T(128)}) while((s32[]{:T(128)}, f32[2,768,1024]{2,1,0:T(8,128)}, s32[16,2]{0,1:T(2,128)S(1)}, f32[16,2,256,256]{3,2,0,1:T(8,128)}, s32[]{:T(128)}, ...), condition=%wide.region_1.2_spmd, body=%wide.region_0.1_spmd.sunk | while | flops 131080 | bytes 2621629 | solution.py:92
  138.7 5.9 %dynamic_update_slice.8 = f32[2,768,1024]{2,1,0:T(8,128)} dynamic-update-slice(f32[2,768,1024]{2,1,0:T(8,128)} %get-tuple-element.210, f32[2,256,256]{2,1,0:T(8,128)S(1)} %bitcast_add_fusion.2, s32[]{:T(128)} %constant.56.clone.1..sunk, s32[]{:T(128)S(6)} %select_n.104, s32[]{:T(128)S(6)} %select_n.105) | dynamic-update-slice | bytes 1048580 | tf_op jit(solution)/shard_map/while/body/eval_jaxpr/dynamic_update_slice | solution.py:88
  150.7 6.7 %dynamic_update_slice.8 = f32[2,768,1024]{2,1,0:T(8,128)} dynamic-update-slice(f32[2,768,1024]{2,1,0:T(8,128)} %get-tuple-element.210, f32[2,256,256]{2,1,0:T(8,128)S(1)} %bitcast_add_fusion.2, s32[]{:T(128)} %constant.56.clone.1..sunk, s32[]{:T(128)S(6)} %select_n.104, s32[]{:T(128)S(6)} %select_n.105) | dynamic-update-slice | bytes 1048580 | tf_op jit(solution)/shard_map/while/body/eval_jaxpr/dynamic_update_slice | solution.py:88
  163.3 5.2 %dynamic_update_slice.8 = f32[2,768,1024]{2,1,0:T(8,128)} dynamic-update-slice(f32[2,768,1024]{2,1,0:T(8,128)} %get-tuple-element.210, f32[2,256,256]{2,1,0:T(8,128)S(1)} %bitcast_add_fusion.2, s32[]{:T(128)} %constant.56.clone.1..sunk, s32[]{:T(128)S(6)} %select_n.104, s32[]{:T(128)S(6)} %select_n.105) | dynamic-update-slice | bytes 1048580 | tf_op jit(solution)/shard_map/while/body/eval_jaxpr/dynamic_update_slice | solution.py:88
  174.5 6.0 %dynamic_update_slice.8 = f32[2,768,1024]{2,1,0:T(8,128)} dynamic-update-slice(f32[2,768,1024]{2,1,0:T(8,128)} %get-tuple-element.210, f32[2,256,256]{2,1,0:T(8,128)S(1)} %bitcast_add_fusion.2, s32[]{:T(128)} %constant.56.clone.1..sunk, s32[]{:T(128)S(6)} %select_n.104, s32[]{:T(128)S(6)} %select_n.105) | dynamic-update-slice | bytes 1048580 | tf_op jit(solution)/shard_map/while/body/eval_jaxpr/dynamic_update_slice | solution.py:88
  186.5 6.5 %dynamic_update_slice.8 = f32[2,768,1024]{2,1,0:T(8,128)} dynamic-update-slice(f32[2,768,1024]{2,1,0:T(8,128)} %get-tuple-element.210, f32[2,256,256]{2,1,0:T(8,128)S(1)} %bitcast_add_fusion.2, s32[]{:T(128)} %constant.56.clone.1..sunk, s32[]{:T(128)S(6)} %select_n.104, s32[]{:T(128)S(6)} %select_n.105) | dynamic-update-slice | bytes 1048580 | tf_op jit(solution)/shard_map/while/body/eval_jaxpr/dynamic_update_slice | solution.py:88
  197.5 1.5 bitcast_add_fusion.2
  199.0 6.5 %dynamic_update_slice.8 = f32[2,768,1024]{2,1,0:T(8,128)} dynamic-update-slice(f32[2,768,1024]{2,1,0:T(8,128)} %get-tuple-element.210, f32[2,256,256]{2,1,0:T(8,128)S(1)} %bitcast_add_fusion.2, s32[]{:T(128)} %constant.56.clone.1..sunk, s32[]{:T(128)S(6)} %select_n.104, s32[]{:T(128)S(6)} %select_n.105) | dynamic-update-slice | bytes 1048580 | tf_op jit(solution)/shard_map/while/body/eval_jaxpr/dynamic_update_slice | solution.py:88
  211.6 6.8 %dynamic_update_slice.8 = f32[2,768,1024]{2,1,0:T(8,128)} dynamic-update-slice(f32[2,768,1024]{2,1,0:T(8,128)} %get-tuple-element.210, f32[2,256,256]{2,1,0:T(8,128)S(1)} %bitcast_add_fusion.2, s32[]{:T(128)} %constant.56.clone.1..sunk, s32[]{:T(128)S(6)} %select_n.104, s32[]{:T(128)S(6)} %select_n.105) | dynamic-update-slice | bytes 1048580 | tf_op jit(solution)/shard_map/while/body/eval_jaxpr/dynamic_update_slice | solution.py:88
  224.3 6.7 %dynamic_update_slice.8 = f32[2,768,1024]{2,1,0:T(8,128)} dynamic-update-slice(f32[2,768,1024]{2,1,0:T(8,128)} %get-tuple-element.210, f32[2,256,256]{2,1,0:T(8,128)S(1)} %bitcast_add_fusion.2, s32[]{:T(128)} %constant.56.clone.1..sunk, s32[]{:T(128)S(6)} %select_n.104, s32[]{:T(128)S(6)} %select_n.105) | dynamic-update-slice | bytes 1048580 | tf_op jit(solution)/shard_map/while/body/eval_jaxpr/dynamic_update_slice | solution.py:88
  237.1 6.6 %dynamic_update_slice.8 = f32[2,768,1024]{2,1,0:T(8,128)} dynamic-update-slice(f32[2,768,1024]{2,1,0:T(8,128)} %get-tuple-element.210, f32[2,256,256]{2,1,0:T(8,128)S(1)} %bitcast_add_fusion.2, s32[]{:T(128)} %constant.56.clone.1..sunk, s32[]{:T(128)S(6)} %select_n.104, s32[]{:T(128)S(6)} %select_n.105) | dynamic-update-slice | bytes 1048580 | tf_op jit(solution)/shard_map/while/body/eval_jaxpr/dynamic_update_slice | solution.py:88
  249.7 6.5 %dynamic_update_slice.8 = f32[2,768,1024]{2,1,0:T(8,128)} dynamic-update-slice(f32[2,768,1024]{2,1,0:T(8,128)} %get-tuple-element.210, f32[2,256,256]{2,1,0:T(8,128)S(1)} %bitcast_add_fusion.2, s32[]{:T(128)} %constant.56.clone.1..sunk, s32[]{:T(128)S(6)} %select_n.104, s32[]{:T(128)S(6)} %select_n.105) | dynamic-update-slice | bytes 1048580 | tf_op jit(solution)/shard_map/while/body/eval_jaxpr/dynamic_update_slice | solution.py:88
  260.7 1.5 bitcast_add_fusion.2
  262.2 6.8 %dynamic_update_slice.8 = f32[2,768,1024]{2,1,0:T(8,128)} dynamic-update-slice(f32[2,768,1024]{2,1,0:T(8,128)} %get-tuple-element.210, f32[2,256,256]{2,1,0:T(8,128)S(1)} %bitcast_add_fusion.2, s32[]{:T(128)} %constant.56.clone.1..sunk, s32[]{:T(128)S(6)} %select_n.104, s32[]{:T(128)S(6)} %select_n.105) | dynamic-update-slice | bytes 1048580 | tf_op jit(solution)/shard_map/while/body/eval_jaxpr/dynamic_update_slice | solution.py:88
  275.0 6.5 %dynamic_update_slice.8 = f32[2,768,1024]{2,1,0:T(8,128)} dynamic-update-slice(f32[2,768,1024]{2,1,0:T(8,128)} %get-tuple-element.210, f32[2,256,256]{2,1,0:T(8,128)S(1)} %bitcast_add_fusion.2, s32[]{:T(128)} %constant.56.clone.1..sunk, s32[]{:T(128)S(6)} %select_n.104, s32[]{:T(128)S(6)} %select_n.105) | dynamic-update-slice | bytes 1048580 | tf_op jit(solution)/shard_map/while/body/eval_jaxpr/dynamic_update_slice | solution.py:88
  287.5 6.3 %dynamic_update_slice.8 = f32[2,768,1024]{2,1,0:T(8,128)} dynamic-update-slice(f32[2,768,1024]{2,1,0:T(8,128)} %get-tuple-element.210, f32[2,256,256]{2,1,0:T(8,128)S(1)} %bitcast_add_fusion.2, s32[]{:T(128)} %constant.56.clone.1..sunk, s32[]{:T(128)S(6)} %select_n.104, s32[]{:T(128)S(6)} %select_n.105) | dynamic-update-slice | bytes 1048580 | tf_op jit(solution)/shard_map/while/body/eval_jaxpr/dynamic_update_slice | solution.py:88
  299.8 6.5 %dynamic_update_slice.8 = f32[2,768,1024]{2,1,0:T(8,128)} dynamic-update-slice(f32[2,768,1024]{2,1,0:T(8,128)} %get-tuple-element.210, f32[2,256,256]{2,1,0:T(8,128)S(1)} %bitcast_add_fusion.2, s32[]{:T(128)} %constant.56.clone.1..sunk, s32[]{:T(128)S(6)} %select_n.104, s32[]{:T(128)S(6)} %select_n.105) | dynamic-update-slice | bytes 1048580 | tf_op jit(solution)/shard_map/while/body/eval_jaxpr/dynamic_update_slice | solution.py:88
  312.3 6.8 %dynamic_update_slice.8 = f32[2,768,1024]{2,1,0:T(8,128)} dynamic-update-slice(f32[2,768,1024]{2,1,0:T(8,128)} %get-tuple-element.210, f32[2,256,256]{2,1,0:T(8,128)S(1)} %bitcast_add_fusion.2, s32[]{:T(128)} %constant.56.clone.1..sunk, s32[]{:T(128)S(6)} %select_n.104, s32[]{:T(128)S(6)} %select_n.105) | dynamic-update-slice | bytes 1048580 | tf_op jit(solution)/shard_map/while/body/eval_jaxpr/dynamic_update_slice | solution.py:88
  325.1 6.5 %dynamic_update_slice.8 = f32[2,768,1024]{2,1,0:T(8,128)} dynamic-update-slice(f32[2,768,1024]{2,1,0:T(8,128)} %get-tuple-element.210, f32[2,256,256]{2,1,0:T(8,128)S(1)} %bitcast_add_fusion.2, s32[]{:T(128)} %constant.56.clone.1..sunk, s32[]{:T(128)S(6)} %select_n.104, s32[]{:T(128)S(6)} %select_n.105) | dynamic-update-slice | bytes 1048580 | tf_op jit(solution)/shard_map/while/body/eval_jaxpr/dynamic_update_slice | solution.py:88
  331.6 3.2 slice.41
  334.8 28.7 %collective-permute-start.1 = (f32[2,256,1024]{2,1,0:T(8,128)}, f32[2,256,1024]{2,1,0:T(8,128)S(1)}, u32[]{:S(2)}, u32[]{:S(2)}) collective-permute-start(f32[2,256,1024]{2,1,0:T(8,128)} %slice.41), channel_id=1, source_target_pairs={{0,1},{1,2},{2,3},{3,4},{4,5},{5,6},{6,7},{7,8},{8,9},{9,10},{10,1... | collective-permute-start | bytes 6291464 | tf_op jit(solution)/shard_map/ppermute | solution.py:12
  364.4 2.9 collective-permute-done.1
  367.3 5.0 %pad_add_fusion = f32[2,512,1024]{2,1,0:T(8,128)} fusion(f32[2,256,1024]{2,1,0:T(8,128)S(1)} %collective-permute-done.1, f32[2,768,1024]{2,1,0:T(8,128)} %get-tuple-element.81), kind=kLoop, calls=%fused_computation.26 | loop fusion | flops 1048576 | bytes 10485760 | tf_op jit(solution)/shard_map/add | solution.py:96
  372.4 83.7 %all-reduce.3.cloned.1.call-done = f32[1,2,256,256]{3,2,1,0:T(8,128)} async-done(((f32[1,2,256,256]{3,2,1,0:T(8,128)}), f32[1,2,256,256]{3,2,1,0:T(8,128)}) %all-reduce.3.cloned.1.call-update) | async-done | bytes 524304 | tf_op jit(solution)/shard_map/psum | solution.py:80
  456.0 1.9 copy.64
  (94 shorter events, 43.9 us)
Async XLA Ops:
  8.0 3.8 copy-start.6
  8.0 3.9 copy-start.3
  8.0 448.0 %all-reduce.3.cloned.1.call-start = ((), (), s32[]{:S(2)}) async-start(), calls=%async_computation.2 | async-start | bytes 1048576 | tf_op jit(solution)/shard_map/psum | solution.py:80
  9.8 6.2 %collective-permute-start = (f32[2,256,1024]{2,1,0:T(8,128)S(1)}, f32[2,256,1024]{2,1,0:T(8,128)}, u32[]{:S(2)}, u32[]{:S(2)}) collective-permute-start(f32[2,256,1024]{2,1,0:T(8,128)S(1)} %slice.34), channel_id=1, source_target_pairs={{1,0},{2,1},{3,2},{4,3},{5,4},{6,5},{7,6},{8,7},{9,8},{10,9},{11,1... | collective-permute-start | bytes 6291464 | tf_op jit(solution)/shard_map/ppermute | solution.py:12
  11.9 74.6 %copy-start.1 = (f32[256,256]{1,0:T(8,128)}, f32[256,256]{1,0:T(8,128)S(1)}, u32[]{:S(2)}) copy-start(f32[256,256]{1,0:T(8,128)S(1)} %get-tuple-element.124) | copy-start | bytes 786436
  11.9 74.5 %copy-start.2 = (f32[256,256]{1,0:T(8,128)}, f32[256,256]{1,0:T(8,128)S(1)}, u32[]{:S(2)}) copy-start(f32[256,256]{1,0:T(8,128)S(1)} %get-tuple-element.125) | copy-start | bytes 786436
  101.3 1.9 copy-start
  114.5 3.4 slice-start
  116.2 2.3 slice-start.1
  331.6 31.9 %copy-start.4 = (f32[256,256]{1,0:T(8,128)S(1)}, f32[256,256]{1,0:T(8,128)}, u32[]{:S(2)}) copy-start(f32[256,256]{1,0:T(8,128)} %get-tuple-element.94) | copy-start | bytes 786436
  331.6 31.9 %copy-start.5 = (f32[256,256]{1,0:T(8,128)S(1)}, f32[256,256]{1,0:T(8,128)}, u32[]{:S(2)}) copy-start(f32[256,256]{1,0:T(8,128)} %get-tuple-element.95) | copy-start | bytes 786436
  334.8 32.5 %collective-permute-start.1 = (f32[2,256,1024]{2,1,0:T(8,128)}, f32[2,256,1024]{2,1,0:T(8,128)S(1)}, u32[]{:S(2)}, u32[]{:S(2)}) collective-permute-start(f32[2,256,1024]{2,1,0:T(8,128)} %slice.41), channel_id=1, source_target_pairs={{0,1},{1,2},{2,3},{3,4},{4,5},{5,6},{6,7},{7,8},{8,9},{9,10},{10,1... | collective-permute-start | bytes 6291464 | tf_op jit(solution)/shard_map/ppermute | solution.py:12
  364.4 91.7 %reduce-scatter.2.cloned.1.call-start = ((), (), s32[]{:S(2)}) async-start(), calls=%async_computation.1 | async-start | bytes 6291456 | tf_op jit(solution)/shard_map/reduce_scatter | solution.py:99
Sparse Core Ops, SparseCore 0:
  364.5 91.5 all-reduce.2
Sparse Core Ops, SparseCore 1:
  372.4 79.3 reduce-scatter.1
where the time goes:
time: 471 us; the launch traced here: 465 us
  local copies, waits for them, and re-layouts  187 us (40%)
  waiting for transfers between devices  90.7 us (19%)
  loops' own time  62.2 us (13%)
  other arithmetic  45.7 us (10%)
  matrix products  33.2 us (7%)
  starting transfers between devices  30 us (6%)
  between operations  16.4 us (3%)
    dynamic_update_slice x16, local copies, waits for them, and re-layouts, accumulate(): lax.dynamic_update_slice(grad_ext, current + obj_terms[slot], (zero_at, r...  103 us
    psum x1, waiting for transfers between devices, on_device(): probe_total = lax.psum(jnp.stack([prb_re, prb_im]), 'region')  83.7 us
    gather x48, local copies, waits for them, and re-layouts  63.8 us
    another operation x1, loops' own time, on_device(): lax.fori_loop(0, slot_total, accumulate, jnp.zeros((2, tile_rows + patch_...  62.2 us
    ppermute x2, starting transfers between devices, from_behind(): return lax.ppermute(block, axis, route)  30 us
    add x16, other arithmetic, accumulate(): current + obj_terms[slot]  24.4 us
    dot_general x8, matrix products, apply_right(): jnp.einsum('bkn,nm->bkm', field_part, table, preferred_element_type=jnp.f...  19.7 us
    dot_general x8, matrix products, apply_left(): jnp.einsum('kn,bnm->bkm', table, field_part, preferred_element_type=jnp.f...  13.5 us
  transfers between devices with their start and end apart: 4, of which 3 were waited for; matrix products, arithmetic and copies ran while one was open for 1% of the time, Pallas kernels for 0%

commit v1 on v0

v1 whole, which is shorter than its diff:
```python
import functools
import math

import jax
import jax.numpy as jnp
import numpy as np
from jax import lax
from jax.experimental import pallas as pl
from jax.experimental.pallas import tpu as pltpu
from jax.sharding import PartitionSpec as P

STRIP = 32
LANES = 128
UNROLL = 2
VMEM_LIMIT = 56 * 1024 * 1024


def from_behind(block, axis, distance):
    devices = range(lax.axis_size(axis))
    route = [(i - distance, i) for i in devices if i - distance in devices]
    return lax.ppermute(block, axis, route)


def make_tables(side):
    index = np.arange(side)
    phase = (index[:, None] * index[None, :] % side) * (2.0 * math.pi / side)
    cos = (np.cos(phase) / math.sqrt(side)).astype(np.float32)
    sin = (np.sin(phase) / math.sqrt(side)).astype(np.float32)
    forward = np.block([[cos, sin], [-sin, cos]])
    inverse = np.block([[cos, -sin], [sin, cos]])
    return jnp.asarray(forward, jnp.bfloat16), jnp.asarray(inverse, jnp.bfloat16)


def patch_kernel(second, side, slots, width, *refs):
    offs, count, field, *refs = refs
    if second:
        rim, grad_in, prb_in, *refs = refs
    probe, patterns, forward, inverse = refs[:4]
    grad, prb = refs[4:6]
    ext, pats, order, sems = refs[6:10]
    patch = refs[10 : 10 + UNROLL]
    wave = refs[10 + UNROLL : 10 + 2 * UNROLL]
    half = refs[10 + 2 * UNROLL : 10 + 3 * UNROLL]
    far = refs[10 + 3 * UNROLL : 10 + 4 * UNROLL]
    base = side if second else 0

    copies = [pltpu.make_async_copy(patterns.at[0], pats, sems.at[0])]
    if second:
        copies += [
            pltpu.make_async_copy(
                grad_in.at[:, :, pl.ds(side, side)], grad.at[:, :, pl.ds(0, side)], sems.at[1]
            ),
        ]
    for k in range(width // LANES):
        cols = pl.ds(k * LANES, LANES)
        if second:
            copies += [
                pltpu.make_async_copy(
                    field.at[:, pl.ds(side, side), cols], ext.at[k, :, pl.ds(0, side)], sems.at[2 + 2 * k]
                ),
                pltpu.make_async_copy(
                    rim.at[:, :, cols], ext.at[k, :, pl.ds(side, side)], sems.at[3 + 2 * k]
                ),
            ]
        else:
            copies += [pltpu.make_async_copy(field.at[:, :, cols], ext.at[k], sems.at[2 + 2 * k])]
    for copy in copies:
        copy.start()

    if second:
        grad[:, :, side:, :] = jnp.zeros((width // LANES, 2, side, LANES), jnp.float32)
        prb[...] = prb_in[...]
    else:
        grad[...] = jnp.zeros_like(grad)
        prb[...] = jnp.zeros_like(prb)

    def gather(slot, found):
        row = offs[slot, 0]
        inside = (row >= side) if second else (row < side)
        take = inside & (slot < count[0])

        @pl.when(take)
        def _():
            order[found] = slot

        return found + take.astype(jnp.int32)

    for lane in range(UNROLL):
        order[slots + lane] = 0
    total = lax.fori_loop(0, slots, gather, jnp.int32(0))
    for lane in range(UNROLL):
        order[total + lane] = 0
    for copy in copies:
        copy.wait()

    chunks = side // LANES
    lane_id = lax.broadcasted_iota(jnp.int32, (STRIP, LANES), 1)

    def place(position):
        slot = order[position]
        row = jnp.clip(offs[slot, 0] - base, 0, side - 1)
        col = offs[slot, 1]
        start = jnp.minimum(col // LANES, width // LANES - chunks - 1)
        return slot, row, start, col - start * LANES

    def body(step, carry):
        placed = [place(step * UNROLL + u) for u in range(UNROLL)]
        for u in range(UNROLL):
            slot, row, start, shift = placed[u]
            back_shift = lax.rem(LANES - shift, LANES)
            for s in range(side // STRIP):
                at = slice(s * STRIP, (s + 1) * STRIP)
                parts = []
                for plane in range(2):
                    rolled = [
                        pltpu.roll(
                            ext[start + k, plane, pl.ds(row + s * STRIP, STRIP), :],
                            back_shift,
                            1,
                        )
                        for k in range(chunks + 1)
                    ]
                    parts.append(
                        [
                            jnp.where(lane_id < LANES - shift, rolled[k], rolled[k + 1])
                            for k in range(chunks)
                        ]
                    )
                for k in range(chunks):
                    cols = slice(k * LANES, (k + 1) * LANES)
                    re, im = parts[0][k], parts[1][k]
                    p_re, p_im = probe[0, 0, at, cols], probe[0, 1, at, cols]
                    patch[u][0, at, cols] = re
                    patch[u][1, at, cols] = im
                    wave[u][at, cols] = (p_re * re - p_im * im).astype(jnp.bfloat16)
                    wave[u][side + s * STRIP : side + (s + 1) * STRIP, cols] = (
                        p_re * im + p_im * re
                    ).astype(jnp.bfloat16)
        for u in range(UNROLL):
            product = jnp.dot(forward[...], wave[u][...], preferred_element_type=jnp.float32)
            half[u][:, :side] = product[:side].astype(jnp.bfloat16)
            half[u][:, side:] = product[side:].astype(jnp.bfloat16)
        for u in range(UNROLL):
            far[u][...] = jnp.dot(half[u][...], inverse[...], preferred_element_type=jnp.float32)
        for u in range(UNROLL):
            slot = placed[u][0]
            for s in range(side // STRIP):
                at = slice(s * STRIP, (s + 1) * STRIP)
                f_re, f_im = far[u][at, :side], far[u][at, side:]
                seen = pats[slot, at, :].astype(jnp.float32)
                excess = f_re * f_re + f_im * f_im - seen
                wave[u][at, :] = (excess * f_re).astype(jnp.bfloat16)
                wave[u][side + s * STRIP : side + (s + 1) * STRIP, :] = (excess * f_im).astype(
                    jnp.bfloat16
                )
        for u in range(UNROLL):
            product = jnp.dot(inverse[...], wave[u][...], preferred_element_type=jnp.float32)
            half[u][:, :side] = product[:side].astype(jnp.bfloat16)
            half[u][:, side:] = product[side:].astype(jnp.bfloat16)
        for u in range(UNROLL):
            far[u][...] = jnp.dot(half[u][...], forward[...], preferred_element_type=jnp.float32)
        for u in range(UNROLL):
            slot, row, start, shift = placed[u]
            valid = (step * UNROLL + u < total).astype(jnp.float32)
            for s in range(side // STRIP):
                at = slice(s * STRIP, (s + 1) * STRIP)
                terms = [[], []]
                for k in range(chunks):
                    cols = slice(k * LANES, (k + 1) * LANES)
                    c_re = far[u][at, cols] * valid
                    c_im = far[u][at, side + k * LANES : side + (k + 1) * LANES] * valid
                    re, im = patch[u][0, at, cols], patch[u][1, at, cols]
                    prb[0, at, cols] += re * c_re + im * c_im
                    prb[1, at, cols] += re * c_im - im * c_re
                    p_re, p_im = probe[0, 0, at, cols], probe[0, 1, at, cols]
                    terms[0].append(p_re * c_re + p_im * c_im)
                    terms[1].append(p_re * c_im - p_im * c_re)
                for plane in range(2):
                    rolled = [pltpu.roll(t, lax.rem(shift, LANES), 1) for t in terms[plane]]
                    rolled = [jnp.zeros_like(rolled[0])] + rolled + [jnp.zeros_like(rolled[0])]
                    for k in range(chunks + 1):
                        where = (start + k, plane, pl.ds(row + s * STRIP, STRIP))
                        grad[where] += jnp.where(lane_id >= shift, rolled[k + 1], rolled[k])
        return carry

    lax.fori_loop(0, (total + UNROLL - 1) // UNROLL, body, 0)


def patch_call(second, offsets, counts, field, extra, probes, patterns, tables):
    side = probes.shape[-1]
    slots = offsets.shape[0]
    width = field.shape[2]
    smem = pl.BlockSpec(memory_space=pltpu.SMEM)
    vmem = pl.BlockSpec(memory_space=pltpu.VMEM)
    hbm = pl.BlockSpec(memory_space=pl.ANY)
    specs = [smem, smem, hbm] + ([hbm, hbm, vmem] if second else []) + [vmem, hbm, vmem, vmem]
    scratch = [
        pltpu.VMEM((width // LANES, 2, 2 * side, LANES), jnp.float32),
        pltpu.VMEM((slots, side, side), jnp.bfloat16),
        pltpu.SMEM((slots + UNROLL,), jnp.int32),
        pltpu.SemaphoreType.DMA((2 + 2 * (width // LANES),)),
    ]
    scratch += [pltpu.VMEM((2, side, side), jnp.float32)] * UNROLL
    scratch += [pltpu.VMEM((2 * side, side), jnp.bfloat16)] * UNROLL
    scratch += [pltpu.VMEM((side, 2 * side), jnp.bfloat16)] * UNROLL
    scratch += [pltpu.VMEM((side, 2 * side), jnp.float32)] * UNROLL
    return pl.pallas_call(
        functools.partial(patch_kernel, second, side, slots, width),
        out_shape=(
            jax.ShapeDtypeStruct((width // LANES, 2, 2 * side, LANES), jnp.float32),
            jax.ShapeDtypeStruct((2, side, side), jnp.float32),
        ),
        in_specs=specs,
        out_specs=(vmem, vmem),
        scratch_shapes=scratch,
        compiler_params=pltpu.CompilerParams(vmem_limit_bytes=VMEM_LIMIT),
        cost_estimate=pl.CostEstimate(
            flops=slots * 16 * side**3, bytes_accessed=20 * 1024 * 1024, transcendentals=0
        ),
        name="second_half" if second else "first_half",
    )(offsets, counts, field, *extra, probes, patterns, *tables)


def wave_sum(block):
    waves = lax.axis_size("wave")
    share = block.shape[0] // waves
    if waves == 2:
        me = lax.axis_index("wave")
        give = lax.dynamic_slice_in_dim(block, (1 - me) * share, share, axis=0)
        keep = lax.dynamic_slice_in_dim(block, me * share, share, axis=0)
        total = keep + lax.ppermute(give, "wave", [(0, 1), (1, 0)])
    else:
        total = lax.psum_scatter(block, "wave", scatter_dimension=0, tiled=True)
    return total.transpose(1, 2, 0, 3).reshape(2, block.shape[2], share * LANES)


def on_device(object_field, probes, patterns, offsets, counts):
    side = probes.shape[-1]
    tables = make_tables(side)
    rim = from_behind(object_field[:, :side, :], "region", -1)
    grad_a, prb_a = patch_call(False, offsets, counts, object_field, (), probes, patterns, tables)
    grad_b, prb_b = patch_call(
        True, offsets, counts, object_field, (rim, grad_a, prb_a), probes, patterns, tables
    )
    arrived = from_behind(grad_b[:, :, side:, :], "region", 1)
    probe_total = lax.psum(prb_b, "region")
    bottom = wave_sum(grad_b[:, :, :side, :])
    top = wave_sum(grad_a[:, :, :side, :] + arrived)
    return (jnp.concatenate([top, bottom], axis=1), probe_total[None])


def solution(mesh):
    in_specs = (
        P(None, "region", None),
        P("wave", None, None, None),
        P("wave", "region", None, None),
        P("region", None),
        P("region"),
    )
    out_specs = (P(None, "region", "wave"), P("wave", None, None, None))
    return jax.shard_map(
        on_device, mesh=mesh, in_specs=in_specs, out_specs=out_specs, check_vma=False
    )
```

time: 471 us -> 190 us (0.40); the launches traced: 465 us -> 189 us
  local copies, waits for them, and re-layouts: 187 us -> 13.8 us
  loops' own time: 62.2 us -> 0 us
  other arithmetic: 45.7 us -> 7.24 us
  matrix products: 33.2 us -> 0 us
  Pallas kernels: 0 us -> 25.3 us
  waiting for transfers between devices: 90.7 us -> 108 us
  starting transfers between devices: 30 us -> 20.3 us
    dynamic_update_slice x16 -> x0, local copies, waits for them, and re-layouts: 103 us -> none  [accumulate(): lax.dynamic_update_slice(grad_ext, current + obj_terms[slot], (zero_at, r...]
    gather x48 -> x0, local copies, waits for them, and re-layouts: 63.8 us -> none
    another operation x2 -> x0, loops' own time: 62.2 us -> none  [the longest x1 62.2 us: on_device(): lax.fori_loop(0, slot_total, accumulate, jnp.zeros((2, tile_rows + patch_...]
    dot_general x16 -> x0, matrix products: 33.2 us -> none  [the longest x8 19.7 us: apply_right(): jnp.einsum('bkn,nm->bkm', field_part, table, preferred_element_type=jnp.f...]
    ppermute x0 -> x2, waiting for transfers between devices: none -> 31.2 us  [wave_sum(): total = keep + lax.ppermute(give, 'wave', [(0, 1), (1, 0)])]
    add x17 -> x1, other arithmetic: 29.4 us -> 2.45 us  [on_device(): top = wave_sum(grad_a[:, :, :side, :] + arrived)]
    pallas_call x0 -> x2, Pallas kernels: none -> 25.3 us  [patch_call(): pl.pallas_call(functools.partial(patch_kernel, second, side, slots, width...]
    ppermute x2, starting transfers between devices: 30 us -> 17.3 us  [from_behind(): return lax.ppermute(block, axis, route)]
  transfers between devices with their start and end apart: 4 -> 5, of which waited for: 3 -> 4; matrix products, arithmetic and copies ran while one was open for 1% -> 7% of each run, Pallas kernels for 0% -> 7%
where the time goes in v1:
time: 190 us; the launch traced here: 189 us
  waiting for transfers between devices  108 us (57%)
  Pallas kernels  25.3 us (13%)
  starting transfers between devices  20.3 us (11%)
  between operations  14.8 us (8%)
  local copies, waits for them, and re-layouts  13.8 us (7%)
  other arithmetic  7.24 us (4%)
    psum x1, waiting for transfers between devices, on_device(): probe_total = lax.psum(prb_b, 'region')  75.4 us
    ppermute x2, waiting for transfers between devices, wave_sum(): total = keep + lax.ppermute(give, 'wave', [(0, 1), (1, 0)])  31.2 us
    pallas_call x2, Pallas kernels, patch_call(): pl.pallas_call(functools.partial(patch_kernel, second, side, slots, width...  25.3 us
    ppermute x2, starting transfers between devices, from_behind(): return lax.ppermute(block, axis, route)  17.3 us
    unnamed x7, local copies, waits for them, and re-layouts  4.37 us
    slice x1, local copies, waits for them, and re-layouts, on_device(): arrived = from_behind(grad_b[:, :, side:, :], 'region', 1)  3.93 us
  transfers between devices with their start and end apart: 5, of which 4 were waited for; matrix products, arithmetic and copies ran while one was open for 7% of the time, Pallas kernels for 7%

profile of v1, /device:TPU:0, one launch (start us, length us, event | category | flops | bytes accessed | tf_op | source)
XLA Modules:
  0.0 189.2 jit_solution(5991946730554396393)
XLA Ops:
  7.2 0.0 copy-start.1
  7.2 0.0 all-reduce.2.cloned.1.call-start
  7.2 1.7 slice.13
  9.0 1.3 collective-permute-start
  10.3 0.0 copy-done.1
  10.3 0.7 copy.11.refs_0_
  11.6 13.4 %first_half.1 = (f32[8,2,512,128]{3,2,1,0:T(8,128)}, f32[2,256,256]{2,1,0:T(8,128)}) custom-call(s32[16,2]{1,0:T(8,128)} %copy.11.refs_0_, s32[1]{0:T(128)S(6)} %copy.17.refs_1_, f32[2,512,1024]{2,1,0:T(8,128)} %refs_2_.3, f32[1,2,256,256]{3,2,1,0:T(8,128)} %refs_6_.2, bf16[1,16,256,256]{3,2,1,0:T(8,128)(2,1)} %refs_7_.1, ...), custom_call_target="tpu_custom_call" | custom-call | flops 4294967296 | bytes 20971520 | tf_op jit(solution)/shard_map/first_half/pallas_call | solution.py:207
  25.0 0.0 collective-permute-done.refs_3_
  25.0 11.9 %second_half.1 = (f32[8,2,512,128]{3,2,1,0:T(8,128)}, f32[2,256,256]{2,1,0:T(8,128)}) custom-call(s32[16,2]{1,0:T(8,128)} %copy.11.refs_0_, s32[1]{0:T(128)S(6)} %copy.17.refs_1_, f32[2,512,1024]{2,1,0:T(8,128)} %refs_2_.3, f32[2,256,1024]{2,1,0:T(8,128)} %collective-permute-done.refs_3_, f32[8,2,512,128]{3,2,1,0:T(8,128)} %get-tuple-element.6.refs_4_, ...), custom_call_target="tpu_custom_call" | custom-call | flops 4294967296 | bytes 20971520 | tf_op jit(solution)/shard_map/second_half/pallas_call | solution.py:207
  37.0 3.9 %fusion = (f32[8,2,256,128]{3,2,1,0:T(8,128)}, f32[8,2,256,128]{3,2,1,0:T(8,128)S(1)}) fusion(f32[8,2,512,128]{3,2,1,0:T(8,128)} %get-tuple-element.8), kind=kLoop, calls=%fused_computation.6 | loop fusion | bytes 8388608 | tf_op jit(solution)/shard_map/slice | solution.py:245
  40.9 0.0 copy-start
  40.9 16.0 %collective-permute-start.1 = (f32[8,2,256,128]{3,2,1,0:T(8,128)}, f32[8,2,256,128]{3,2,1,0:T(8,128)}, u32[]{:S(2)}, u32[]{:S(2)}) collective-permute-start(f32[8,2,256,128]{3,2,1,0:T(8,128)} %get-tuple-element.12), channel_id=1, source_target_pairs={{0,1},{1,2},{2,3},{3,4},{4,5},{5,6},{6,7},{7,8},{8,9},{9,10},{10,1... | collective-permute-start | bytes 6291464 | tf_op jit(solution)/shard_map/ppermute | solution.py:21
  56.9 0.1 constant_dynamic-slice_fusion
  56.9 1.6 collective-permute-start.3
  58.5 0.0 copy-done
  58.5 1.1 collective-permute-done.1
  59.6 2.4 %slice_add_fusion = f32[8,2,256,128]{3,2,1,0:T(8,128)S(1)} fusion(f32[8,2,256,128]{3,2,1,0:T(8,128)} %collective-permute-done.1, f32[8,2,512,128]{3,2,1,0:T(8,128)} %get-tuple-element.6.refs_4_), kind=kLoop, calls=%fused_computation.1 | loop fusion | flops 524288 | bytes 6291456 | tf_op jit(solution)/shard_map/add | solution.py:248
  62.1 1.1 constant_dynamic-slice_fusion.1
  63.1 1.5 collective-permute-start.2
  64.6 0.0 all-reduce.2.cloned.1.call-update
  64.7 16.2 %collective-permute-done.3 = f32[4,2,256,128]{3,2,1,0:T(8,128)} collective-permute-done((f32[4,2,256,128]{3,2,1,0:T(8,128)S(1)}, f32[4,2,256,128]{3,2,1,0:T(8,128)}, u32[]{:S(2)}, u32[]{:S(2)}) %collective-permute-start.3) | collective-permute-done | bytes 1048608 | tf_op jit(solution)/shard_map/ppermute | solution.py:231
  80.9 1.6 add_bitcast_fusion
  82.5 1.3 copy.14
  83.8 15.1 %collective-permute-done.2 = f32[4,2,256,128]{3,2,1,0:T(8,128)} collective-permute-done((f32[4,2,256,128]{3,2,1,0:T(8,128)}, f32[4,2,256,128]{3,2,1,0:T(8,128)}, u32[]{:S(2)}, u32[]{:S(2)}) %collective-permute-start.2) | collective-permute-done | bytes 1048608 | tf_op jit(solution)/shard_map/ppermute | solution.py:231
  98.9 1.3 add_bitcast_fusion.1
  100.2 1.3 copy.13
  101.5 1.8 pad_maximum_fusion
  103.3 1.8 copy.15
  105.1 75.4 %all-reduce.2.cloned.1.call-done = f32[1,2,256,256]{3,2,1,0:T(8,128)} async-done(((f32[1,2,256,256]{3,2,1,0:T(8,128)}), f32[1,2,256,256]{3,2,1,0:T(8,128)}) %all-reduce.2.cloned.1.call-update) | async-done | bytes 524304 | tf_op jit(solution)/shard_map/psum | solution.py:246
  180.5 1.9 copy.18
Async XLA Ops:
  7.2 3.1 %copy-start.1 = (s32[16,2]{0,1:T(2,128)S(1)}, s32[16,2]{0,1:T(2,128)}, u32[]{:S(2)}) copy-start(s32[16,2]{0,1:T(2,128)} %param.10) | copy-start | bytes 388
  7.2 173.4 %all-reduce.2.cloned.1.call-start = ((), (), s32[]{:S(2)}) async-start(), calls=%async_computation | async-start | bytes 1048576 | tf_op jit(solution)/shard_map/psum | solution.py:246
  9.0 16.1 %collective-permute-start = (f32[2,256,1024]{2,1,0:T(8,128)S(1)}, f32[2,256,1024]{2,1,0:T(8,128)}, u32[]{:S(2)}, u32[]{:S(2)}) collective-permute-start(f32[2,256,1024]{2,1,0:T(8,128)S(1)} %slice.13), channel_id=1, source_target_pairs={{1,0},{2,1},{3,2},{4,3},{5,4},{6,5},{7,6},{8,7},{9,8},{10,9},{11,1... | collective-permute-start | bytes 6291464 | tf_op jit(solution)/shard_map/ppermute | solution.py:21
  40.9 17.6 %copy-start = (f32[8,2,256,128]{3,2,1,0:T(8,128)}, f32[8,2,256,128]{3,2,1,0:T(8,128)S(1)}, u32[]{:S(2)}) copy-start(f32[8,2,256,128]{3,2,1,0:T(8,128)S(1)} %get-tuple-element.13) | copy-start | bytes 6291460
  40.9 18.7 %collective-permute-start.1 = (f32[8,2,256,128]{3,2,1,0:T(8,128)}, f32[8,2,256,128]{3,2,1,0:T(8,128)}, u32[]{:S(2)}, u32[]{:S(2)}) collective-permute-start(f32[8,2,256,128]{3,2,1,0:T(8,128)} %get-tuple-element.12), channel_id=1, source_target_pairs={{0,1},{1,2},{2,3},{3,4},{4,5},{5,6},{6,7},{7,8},{8,9},{9,10},{10,1... | collective-permute-start | bytes 6291464 | tf_op jit(solution)/shard_map/ppermute | solution.py:21
  56.9 23.9 %collective-permute-start.3 = (f32[4,2,256,128]{3,2,1,0:T(8,128)S(1)}, f32[4,2,256,128]{3,2,1,0:T(8,128)}, u32[]{:S(2)}, u32[]{:S(2)}) collective-permute-start(f32[4,2,256,128]{3,2,1,0:T(8,128)S(1)} %constant_dynamic-slice_fusion), channel_id=1, source_target_pairs={{0,16},{16,0},{1,17},{17,1},{2,18},{18,2},{3,19},{19,3},{4,20},{20... | collective-permute-start | bytes 3145736 | tf_op jit(solution)/shard_map/ppermute | solution.py:231
  63.1 35.7 %collective-permute-start.2 = (f32[4,2,256,128]{3,2,1,0:T(8,128)}, f32[4,2,256,128]{3,2,1,0:T(8,128)}, u32[]{:S(2)}, u32[]{:S(2)}) collective-permute-start(f32[4,2,256,128]{3,2,1,0:T(8,128)} %constant_dynamic-slice_fusion.1), channel_id=1, source_target_pairs={{0,16},{16,0},{1,17},{17,1},{2,18},{18,2},{3,19},{19,3},{4,20},{20... | collective-permute-start | bytes 3145736 | tf_op jit(solution)/shard_map/ppermute | solution.py:231
Sparse Core Ops, SparseCore 0:
  64.8 115.6 all-reduce.1

commit v2 on v1

--- a/solution.py
+++ b/solution.py
@@ -221,27 +221,210 @@
     )(offsets, counts, field, *extra, probes, patterns, *tables)
 
 
+def exchange_kernel(waves, regions, a_ref, b_ref, prb_ref, out, total, *scratch):
+    halo, low_in, top_in, top_out, a_top, b_low, acc, full, *rest = scratch
+    bits = regions.bit_length() - 1
+    stages, (local_sem, halo_send, halo_recv, low_sem, top_send, top_recv, rs_sem, ag_sem) = (
+        rest[:bits],
+        rest[bits:],
+    )
+    side = a_top.shape[2]
+    share = b_low.shape[0]
+    me = lax.axis_index("region")
+    wave = lax.axis_index("wave")
+    mine, other = wave * share, (1 - wave) * share
+    first, last = me == 0, me == regions - 1
+
+    def remote(src, dst, send, recv, axis, target):
+        return pltpu.make_async_remote_copy(
+            src_ref=src,
+            dst_ref=dst,
+            send_sem=send,
+            recv_sem=recv,
+            device_id={axis: target},
+            device_id_type=pl.DeviceIdType.MESH,
+        )
+
+    def flipped(bit):
+        value = lax.rem(me // (1 << bit), 2)
+        return value, me + (1 - 2 * value) * (1 << bit)
+
+    locals_ = [
+        pltpu.make_async_copy(prb_ref, acc, local_sem.at[0]),
+        pltpu.make_async_copy(a_ref.at[:, :, pl.ds(0, side)], a_top, local_sem.at[1]),
+        pltpu.make_async_copy(
+            b_ref.at[pl.ds(mine, share), :, pl.ds(0, side)], b_low, local_sem.at[2]
+        ),
+    ]
+    for copy in locals_:
+        copy.start()
+
+    @pl.when(first)
+    def _():
+        halo[...] = jnp.zeros_like(halo)
+
+    barrier = pltpu.get_barrier_semaphore()
+
+    def greet(axis, target):
+        pl.semaphore_signal(
+            barrier, inc=1, device_id={axis: target}, device_id_type=pl.DeviceIdType.MESH
+        )
+
+    greet("wave", 1 - wave)
+    for bit in range(bits):
+        greet("region", flipped(bit)[1])
+    greet("region", lax.rem(me + 1, regions))
+    greet("region", lax.rem(me + regions - 1, regions))
+    pl.semaphore_wait(barrier, 3 + bits)
+
+    def halo_copy(chunk, count, sem):
+        return remote(
+            b_ref.at[pl.ds(chunk, count), :, pl.ds(side, side)],
+            halo.at[pl.ds(chunk, count)],
+            halo_send.at[sem],
+            halo_recv.at[sem],
+            "region",
+            lax.rem(me + 1, regions),
+        )
+
+    halo_copies = [halo_copy(other + j, 1, j) for j in range(share)] + [halo_copy(mine, share, share)]
+
+    @pl.when(jnp.logical_not(last))
+    def _():
+        halo_copies[0].start()
+
+    low = remote(
+        b_ref.at[pl.ds(other, share), :, pl.ds(0, side)],
+        low_in,
+        low_sem.at[0],
+        low_sem.at[1],
+        "wave",
+        1 - wave,
+    )
+    low.start()
+
+    @pl.when(jnp.logical_not(last))
+    def _():
+        for copy in halo_copies[1:]:
+            copy.start()
+
+    for copy in locals_:
+        copy.wait()
+
+    start, size = jnp.int32(0), acc.shape[0]
+    for bit in range(bits):
+        value, target = flipped(bit)
+        size //= 2
+        give = pl.multiple_of(start + (1 - value) * size, 8)
+        start = pl.multiple_of(start + value * size, 8)
+        copy = remote(
+            acc.at[pl.ds(give, size)],
+            stages[bit],
+            rs_sem.at[0, bit],
+            rs_sem.at[1, bit],
+            "region",
+            target,
+        )
+        copy.start()
+        copy.wait()
+        acc[pl.ds(start, size), :] += stages[bit][...]
+    full[pl.ds(start, size), :] = acc[pl.ds(start, size), :]
+
+    tops = []
+    for j in range(share):
+        pl.when(jnp.logical_not(first))(lambda j=j: halo_copies[j].wait_recv())
+        top_out[j] = a_top[other + j] + halo[other + j]
+        copy = remote(
+            top_out.at[j], top_in.at[j], top_send.at[j], top_recv.at[j], "wave", 1 - wave
+        )
+        copy.start()
+        tops.append(copy)
+
+    for bit in reversed(range(bits)):
+        value, target = flipped(bit)
+        copy = remote(
+            full.at[pl.ds(start, size)],
+            full.at[pl.ds(start, size)],
+            ag_sem.at[0, bit],
+            ag_sem.at[1, bit],
+            "region",
+            target,
+        )
+        copy.start()
+        copy.wait()
+        start = pl.multiple_of(start - value * size, 8)
+        size *= 2
+    total[...] = full[...]
+
+    pl.when(jnp.logical_not(first))(lambda: halo_copies[share].wait_recv())
+    low.wait()
+    for j in range(share):
+        cols = slice(j * LANES, (j + 1) * LANES)
+        out[:, side:, cols] = b_low[j] + low_in[j]
+        a_top[mine + j] = a_top[mine + j] + halo[mine + j]
+    for j in range(share):
+        cols = slice(j * LANES, (j + 1) * LANES)
+        tops[j].wait()
+        out[:, :side, cols] = a_top[mine + j] + top_in[j]
+
+    @pl.when(jnp.logical_not(last))
+    def _():
+        for copy in halo_copies:
+            copy.wait_send()
+
+
+def exchange_call(grad_a, grad_b, prb, waves, regions):
+    chunks, planes, double, _ = grad_a.shape
+    side, share = double // 2, chunks // waves
+    bits = regions.bit_length() - 1
+    vmem = pl.BlockSpec(memory_space=pltpu.VMEM)
+    hbm = pl.BlockSpec(memory_space=pl.ANY)
+    f32 = jnp.float32
+    rows = planes * side
+
+    def block(count):
+        return pltpu.VMEM((count, planes, side, LANES), f32)
+
+    scratch = [block(chunks), block(share), block(share), block(share), block(chunks), block(share)]
+    scratch += [pltpu.VMEM((rows, side), f32)] * 2
+    scratch += [pltpu.VMEM((rows >> (bit + 1), side), f32) for bit in range(bits)]
+    dma = pltpu.SemaphoreType.DMA
+    scratch += [dma((3,)), dma((share + 1,)), dma((share + 1,)), dma((2,))]
+    scratch += [dma((share,)), dma((share,)), dma((2, bits)), dma((2, bits))]
+    return pl.pallas_call(
+        functools.partial(exchange_kernel, waves, regions),
+        out_shape=(
+            jax.ShapeDtypeStruct((planes, double, share * LANES), f32),
+            jax.ShapeDtypeStruct((rows, side), f32),
+        ),
+        in_specs=[hbm, hbm, hbm],
+        out_specs=(vmem, vmem),
+        scratch_shapes=scratch,
+        compiler_params=pltpu.CompilerParams(
+            vmem_limit_bytes=VMEM_LIMIT, collective_id=0, has_side_effects=True
+        ),
+        name="exchange",
+    )(grad_a, grad_b, prb.reshape(rows, side))
+
+
 def wave_sum(block):
-    waves = lax.axis_size("wave")
-    share = block.shape[0] // waves
-    if waves == 2:
-        me = lax.axis_index("wave")
-        give = lax.dynamic_slice_in_dim(block, (1 - me) * share, share, axis=0)
-        keep = lax.dynamic_slice_in_dim(block, me * share, share, axis=0)
-        total = keep + lax.ppermute(give, "wave", [(0, 1), (1, 0)])
-    else:
-        total = lax.psum_scatter(block, "wave", scatter_dimension=0, tiled=True)
+    share = block.shape[0] // lax.axis_size("wave")
+    total = lax.psum_scatter(block, "wave", scatter_dimension=0, tiled=True)
     return total.transpose(1, 2, 0, 3).reshape(2, block.shape[2], share * LANES)
 
 
 def on_device(object_field, probes, patterns, offsets, counts):
     side = probes.shape[-1]
+    waves, regions = lax.axis_size("wave"), lax.axis_size("region")
     tables = make_tables(side)
     rim = from_behind(object_field[:, :side, :], "region", -1)
     grad_a, prb_a = patch_call(False, offsets, counts, object_field, (), probes, patterns, tables)
     grad_b, prb_b = patch_call(
         True, offsets, counts, object_field, (rim, grad_a, prb_a), probes, patterns, tables
     )
+    if waves == 2 and regions & (regions - 1) == 0:
+        object_out, probe_total = exchange_call(grad_a, grad_b, prb_b, waves, regions)
+        return (object_out, probe_total.reshape((1,) + prb_b.shape))
     arrived = from_behind(grad_b[:, :, side:, :], "region", 1)
     probe_total = lax.psum(prb_b, "region")
     bottom = wave_sum(grad_b[:, :, :side, :])

time: 190 us -> 114 us (0.60); the launches traced: 189 us -> 115 us
  waiting for transfers between devices: 108 us -> 0.01 us
  Pallas kernels: 25.3 us -> 106 us
  starting transfers between devices: 20.3 us -> 1.29 us
  between operations: 14.8 us -> 1.34 us
  local copies, waits for them, and re-layouts: 13.8 us -> 6.34 us
  other arithmetic: 7.24 us -> 0 us
    pallas_call x0 -> x1, Pallas kernels: none -> 78.7 us  [exchange_call(): pl.pallas_call(functools.partial(exchange_kernel, waves, regions), out_sh...]
    psum x1 -> x0, waiting for transfers between devices: 75.4 us -> none  [on_device(): probe_total = lax.psum(prb_b, 'region')]
    ppermute x2 -> x0, waiting for transfers between devices: 31.2 us -> none  [wave_sum(): total = keep + lax.ppermute(give, 'wave', [(0, 1), (1, 0)])]
    ppermute x2 -> x1, starting transfers between devices: 17.3 us -> 1.29 us  [from_behind(): return lax.ppermute(block, axis, route)]
    slice x1 -> x0, local copies, waits for them, and re-layouts: 3.93 us -> none  [on_device(): arrived = from_behind(grad_b[:, :, side:, :], 'region', 1)]
    ppermute x2 -> x0, starting transfers between devices: 3.05 us -> none  [wave_sum(): total = keep + lax.ppermute(give, 'wave', [(0, 1), (1, 0)])]
    transpose x2 -> x0, other arithmetic: 2.99 us -> none  [wave_sum(): return total.transpose(1, 2, 0, 3).reshape(2, block.shape[2], share * LANES)]
    transpose x2 -> x0, local copies, waits for them, and re-layouts: 2.61 us -> none  [wave_sum(): return total.transpose(1, 2, 0, 3).reshape(2, block.shape[2], share * LANES)]
  transfers between devices with their start and end apart: 5 -> 1, of which waited for: 4 -> 0; matrix products, arithmetic and copies ran while one was open for 7% -> 1% of each run, Pallas kernels for 7% -> 10%
where the time goes in v2:
time: 114 us; the launch traced here: 115 us
  Pallas kernels  106 us (93%)
  local copies, waits for them, and re-layouts  6.34 us (6%)
  between operations  1.34 us (1%)
  starting transfers between devices  1.29 us (1%)
    pallas_call x1, Pallas kernels, exchange_call(): pl.pallas_call(functools.partial(exchange_kernel, waves, regions), out_sh...  78.7 us
    pallas_call x2, Pallas kernels, patch_call(): pl.pallas_call(functools.partial(patch_kernel, second, side, slots, width...  27.6 us
    unnamed x7, local copies, waits for them, and re-layouts  4.61 us
  transfers between devices with their start and end apart: 1, of which 0 were waited for; matrix products, arithmetic and copies ran while one was open for 1% of the time, Pallas kernels for 10%

profile of v2, /device:TPU:0, one launch (start us, length us, event | category | flops | bytes accessed | tf_op | source)
XLA Modules:
  0.0 115.3 jit_solution(18135794378032554782)
XLA Ops:
  0.6 0.0 copy-start.1
  0.6 1.7 %slice.3 = f32[2,256,1024]{2,1,0:T(8,128)S(1)} slice(f32[2,512,1024]{2,1,0:T(8,128)} %refs_2_.3), slice={[0:2], [0:256], [0:1024]} | slice | bytes 4194304 | tf_op jit(solution)/shard_map/slice | solution.py:420
  2.4 1.3 %collective-permute-start = (f32[2,256,1024]{2,1,0:T(8,128)S(1)}, f32[2,256,1024]{2,1,0:T(8,128)}, u32[]{:S(2)}, u32[]{:S(2)}) collective-permute-start(f32[2,256,1024]{2,1,0:T(8,128)S(1)} %slice.3), channel_id=1, source_target_pairs={{1,0},{2,1},{3,2},{4,3},{5,4},{6,5},{7,6},{8,7},{9,8},{10,9},{11,1... | collective-permute-start | bytes 6291464 | tf_op jit(solution)/shard_map/ppermute | solution.py:21
  4.3 0.0 copy-done.1
  4.3 0.7 copy.9.refs_0_
  5.0 11.1 %first_half.1 = (f32[8,2,512,128]{3,2,1,0:T(8,128)}, f32[2,256,256]{2,1,0:T(8,128)}) custom-call(s32[16,2]{1,0:T(8,128)} %copy.9.refs_0_, s32[1]{0:T(128)S(6)} %copy.13.refs_1_, f32[2,512,1024]{2,1,0:T(8,128)} %refs_2_.3, f32[1,2,256,256]{3,2,1,0:T(8,128)} %refs_6_.2, bf16[1,16,256,256]{3,2,1,0:T(8,128)(2,1)} %refs_7_.1, ...), custom_call_target="tpu_custom_call" | custom-call | flops 4294967296 | bytes 20971520 | tf_op jit(solution)/shard_map/first_half/pallas_call | solution.py:207
  16.1 0.0 collective-permute-done.refs_3_
  16.1 16.5 %second_half.1 = (f32[8,2,512,128]{3,2,1,0:T(8,128)}, f32[2,256,256]{2,1,0:T(8,128)}) custom-call(s32[16,2]{1,0:T(8,128)} %copy.9.refs_0_, s32[1]{0:T(128)S(6)} %copy.13.refs_1_, f32[2,512,1024]{2,1,0:T(8,128)} %refs_2_.3, f32[2,256,1024]{2,1,0:T(8,128)} %collective-permute-done.refs_3_, f32[8,2,512,128]{3,2,1,0:T(8,128)} %get-tuple-element.8.refs_4_.a_ref, ...), custom_call_target="tpu_custom_call" | custom-call | flops 4294967296 | bytes 20971520 | tf_op jit(solution)/shard_map/second_half/pallas_call | solution.py:207
  32.7 78.7 %exchange.1 = (f32[2,512,512]{2,1,0:T(8,128)}, f32[512,256]{1,0:T(8,128)}) custom-call(f32[8,2,512,128]{3,2,1,0:T(8,128)} %get-tuple-element.8.refs_4_.a_ref, f32[8,2,512,128]{3,2,1,0:T(8,128)} %get-tuple-element.10.b_ref, f32[512,256]{1,0:T(8,128)} %bitcast.2), custom_call_target="tpu_custom_call" | custom-call | tf_op jit(solution)/shard_map/exchange/pallas_call | solution.py:394
  111.4 0.0 copy-start
  111.4 3.1 %copy.14 = f32[2,512,512]{2,1,0:T(8,128)} copy(f32[2,512,512]{2,1,0:T(8,128)} %get-tuple-element.16) | data formatting | bytes 4194304
  114.5 0.0 copy-done
  114.5 0.8 copy.15
Async XLA Ops:
  0.6 3.7 %copy-start.1 = (s32[16,2]{0,1:T(2,128)S(1)}, s32[16,2]{0,1:T(2,128)}, u32[]{:S(2)}) copy-start(s32[16,2]{0,1:T(2,128)} %param.10) | copy-start | bytes 388
  2.4 13.7 %collective-permute-start = (f32[2,256,1024]{2,1,0:T(8,128)S(1)}, f32[2,256,1024]{2,1,0:T(8,128)}, u32[]{:S(2)}, u32[]{:S(2)}) collective-permute-start(f32[2,256,1024]{2,1,0:T(8,128)S(1)} %slice.3), channel_id=1, source_target_pairs={{1,0},{2,1},{3,2},{4,3},{5,4},{6,5},{7,6},{8,7},{9,8},{10,9},{11,1... | collective-permute-start | bytes 6291464 | tf_op jit(solution)/shard_map/ppermute | solution.py:21
  111.4 3.1 %copy-start = (f32[512,256]{1,0:T(8,128)S(1)}, f32[512,256]{1,0:T(8,128)}, u32[]{:S(2)}) copy-start(f32[512,256]{1,0:T(8,128)} %get-tuple-element.13) | copy-start | bytes 1572868

commit v3 on v2

--- a/solution.py
+++ b/solution.py
@@ -12,7 +12,10 @@
 STRIP = 32
 LANES = 128
 UNROLL = 2
-VMEM_LIMIT = 56 * 1024 * 1024
+PATCH_VMEM = 28 * 1024 * 1024
+EXCHANGE_VMEM = 20 * 1024 * 1024
+RIM_VMEM = 8 * 1024 * 1024
+PIECES = 4
 
 
 def from_behind(block, axis, distance):
@@ -31,10 +34,8 @@
     return jnp.asarray(forward, jnp.bfloat16), jnp.asarray(inverse, jnp.bfloat16)
 
 
-def patch_kernel(second, side, slots, width, *refs):
-    offs, count, field, *refs = refs
-    if second:
-        rim, grad_in, prb_in, *refs = refs
+def patch_kernel(side, tile, slots, width, *refs):
+    offs, count, field, rim, *refs = refs
     probe, patterns, forward, inverse = refs[:4]
     grad, prb = refs[4:6]
     ext, pats, order, sems = refs[6:10]
@@ -42,42 +43,22 @@
     wave = refs[10 + UNROLL : 10 + 2 * UNROLL]
     half = refs[10 + 2 * UNROLL : 10 + 3 * UNROLL]
     far = refs[10 + 3 * UNROLL : 10 + 4 * UNROLL]
-    base = side if second else 0
-
-    copies = [pltpu.make_async_copy(patterns.at[0], pats, sems.at[0])]
-    if second:
-        copies += [
-            pltpu.make_async_copy(
-                grad_in.at[:, :, pl.ds(side, side)], grad.at[:, :, pl.ds(0, side)], sems.at[1]
-            ),
-        ]
+
+    copies = []
     for k in range(width // LANES):
         cols = pl.ds(k * LANES, LANES)
-        if second:
-            copies += [
-                pltpu.make_async_copy(
-                    field.at[:, pl.ds(side, side), cols], ext.at[k, :, pl.ds(0, side)], sems.at[2 + 2 * k]
-                ),
-                pltpu.make_async_copy(
-                    rim.at[:, :, cols], ext.at[k, :, pl.ds(side, side)], sems.at[3 + 2 * k]
-                ),
-            ]
-        else:
-            copies += [pltpu.make_async_copy(field.at[:, :, cols], ext.at[k], sems.at[2 + 2 * k])]
+        copies += [
+            pltpu.make_async_copy(field.at[:, :, cols], ext.at[k, :, pl.ds(0, tile)], sems.at[2 * k]),
+            pltpu.make_async_copy(rim.at[:, :, cols], ext.at[k, :, pl.ds(tile, side)], sems.at[2 * k + 1]),
+        ]
+    copies += [pltpu.make_async_copy(patterns.at[0], pats, sems.at[2 * (width // LANES)])]
     for copy in copies:
         copy.start()
-
-    if second:
-        grad[:, :, side:, :] = jnp.zeros((width // LANES, 2, side, LANES), jnp.float32)
-        prb[...] = prb_in[...]
-    else:
-        grad[...] = jnp.zeros_like(grad)
-        prb[...] = jnp.zeros_like(prb)
+    grad[...] = jnp.zeros_like(grad)
+    prb[...] = jnp.zeros_like(prb)
 
     def gather(slot, found):
-        row = offs[slot, 0]
-        inside = (row >= side) if second else (row < side)
-        take = inside & (slot < count[0])
+        take = slot < count[0]
 
         @pl.when(take)
         def _():
@@ -98,7 +79,7 @@
 
     def place(position):
         slot = order[position]
-        row = jnp.clip(offs[slot, 0] - base, 0, side - 1)
+        row = offs[slot, 0]
         col = offs[slot, 1]
         start = jnp.minimum(col // LANES, width // LANES - chunks - 1)
         return slot, row, start, col - start * LANES
@@ -186,42 +167,42 @@
     lax.fori_loop(0, (total + UNROLL - 1) // UNROLL, body, 0)
 
 
-def patch_call(second, offsets, counts, field, extra, probes, patterns, tables):
+def patch_call(offsets, counts, field, rim, probes, patterns, tables):
     side = probes.shape[-1]
     slots = offsets.shape[0]
-    width = field.shape[2]
+    tile, width = field.shape[1:]
     smem = pl.BlockSpec(memory_space=pltpu.SMEM)
     vmem = pl.BlockSpec(memory_space=pltpu.VMEM)
     hbm = pl.BlockSpec(memory_space=pl.ANY)
-    specs = [smem, smem, hbm] + ([hbm, hbm, vmem] if second else []) + [vmem, hbm, vmem, vmem]
+    specs = [smem, smem, hbm, hbm, vmem, hbm, vmem, vmem]
     scratch = [
-        pltpu.VMEM((width // LANES, 2, 2 * side, LANES), jnp.float32),
+        pltpu.VMEM((width // LANES, 2, tile + side, LANES), jnp.float32),
         pltpu.VMEM((slots, side, side), jnp.bfloat16),
         pltpu.SMEM((slots + UNROLL,), jnp.int32),
-        pltpu.SemaphoreType.DMA((2 + 2 * (width // LANES),)),
+        pltpu.SemaphoreType.DMA((1 + 2 * (width // LANES),)),
     ]
     scratch += [pltpu.VMEM((2, side, side), jnp.float32)] * UNROLL
     scratch += [pltpu.VMEM((2 * side, side), jnp.bfloat16)] * UNROLL
     scratch += [pltpu.VMEM((side, 2 * side), jnp.bfloat16)] * UNROLL
     scratch += [pltpu.VMEM((side, 2 * side), jnp.float32)] * UNROLL
     return pl.pallas_call(
-        functools.partial(patch_kernel, second, side, slots, width),
+        functools.partial(patch_kernel, side, tile, slots, width),
         out_shape=(
-            jax.ShapeDtypeStruct((width // LANES, 2, 2 * side, LANES), jnp.float32),
+            jax.ShapeDtypeStruct((width // LANES, 2, tile + side, LANES), jnp.float32),
             jax.ShapeDtypeStruct((2, side, side), jnp.float32),
         ),
         in_specs=specs,
         out_specs=(vmem, vmem),
         scratch_shapes=scratch,
-        compiler_params=pltpu.CompilerParams(vmem_limit_bytes=VMEM_LIMIT),
+        compiler_params=pltpu.CompilerParams(vmem_limit_bytes=PATCH_VMEM),
         cost_estimate=pl.CostEstimate(
             flops=slots * 16 * side**3, bytes_accessed=20 * 1024 * 1024, transcendentals=0
         ),
-        name="second_half" if second else "first_half",
-    )(offsets, counts, field, *extra, probes, patterns, *tables)
-
-
-def exchange_kernel(waves, regions, a_ref, b_ref, prb_ref, out, total, *scratch):
+        name="patches",
+    )(offsets, counts, field, rim, probes, patterns, *tables)
+
+
+def exchange_kernel(regions, grad_ref, prb_ref, out, total, *scratch):
     halo, low_in, top_in, top_out, a_top, b_low, acc, full, *rest = scratch
     bits = regions.bit_length() - 1
     stages, (local_sem, halo_send, halo_recv, low_sem, top_send, top_recv, rs_sem, ag_sem) = (
@@ -229,6 +210,7 @@
         rest[bits:],
     )
     side = a_top.shape[2]
+    tile = grad_ref.shape[2] - side
     share = b_low.shape[0]
     me = lax.axis_index("region")
     wave = lax.axis_index("wave")
@@ -251,9 +233,9 @@
 
     locals_ = [
         pltpu.make_async_copy(prb_ref, acc, local_sem.at[0]),
-        pltpu.make_async_copy(a_ref.at[:, :, pl.ds(0, side)], a_top, local_sem.at[1]),
+        pltpu.make_async_copy(grad_ref.at[:, :, pl.ds(0, side)], a_top, local_sem.at[1]),
         pltpu.make_async_copy(
-            b_ref.at[pl.ds(mine, share), :, pl.ds(0, side)], b_low, local_sem.at[2]
+            grad_ref.at[pl.ds(mine, share), :, pl.ds(side, tile - side)], b_low, local_sem.at[2]
         ),
     ]
     for copy in locals_:
@@ -279,7 +261,7 @@
 
     def halo_copy(chunk, count, sem):
         return remote(
-            b_ref.at[pl.ds(chunk, count), :, pl.ds(side, side)],
+            grad_ref.at[pl.ds(chunk, count), :, pl.ds(tile, side)],
             halo.at[pl.ds(chunk, count)],
             halo_send.at[sem],
             halo_recv.at[sem],
@@ -294,7 +276,7 @@
         halo_copies[0].start()
 
     low = remote(
-        b_ref.at[pl.ds(other, share), :, pl.ds(0, side)],
+        grad_ref.at[pl.ds(other, share), :, pl.ds(side, tile - side)],
         low_in,
         low_sem.at[0],
         low_sem.at[1],
@@ -373,38 +355,40 @@
             copy.wait_send()
 
 
-def exchange_call(grad_a, grad_b, prb, waves, regions):
-    chunks, planes, double, _ = grad_a.shape
-    side, share = double // 2, chunks // waves
+def exchange_call(grad, prb, waves, regions):
+    chunks, planes, all_rows, _ = grad.shape
+    side, share = prb.shape[-1], chunks // waves
+    tile = all_rows - side
     bits = regions.bit_length() - 1
     vmem = pl.BlockSpec(memory_space=pltpu.VMEM)
     hbm = pl.BlockSpec(memory_space=pl.ANY)
     f32 = jnp.float32
     rows = planes * side
 
-    def block(count):
-        return pltpu.VMEM((count, planes, side, LANES), f32)
-
-    scratch = [block(chunks), block(share), block(share), block(share), block(chunks), block(share)]
+    def block(count, height):
+        return pltpu.VMEM((count, planes, height, LANES), f32)
+
+    scratch = [block(chunks, side), block(share, tile - side), block(share, side)]
+    scratch += [block(share, side), block(chunks, side), block(share, tile - side)]
     scratch += [pltpu.VMEM((rows, side), f32)] * 2
     scratch += [pltpu.VMEM((rows >> (bit + 1), side), f32) for bit in range(bits)]
     dma = pltpu.SemaphoreType.DMA
     scratch += [dma((3,)), dma((share + 1,)), dma((share + 1,)), dma((2,))]
     scratch += [dma((share,)), dma((share,)), dma((2, bits)), dma((2, bits))]
     return pl.pallas_call(
-        functools.partial(exchange_kernel, waves, regions),
+        functools.partial(exchange_kernel, regions),
         out_shape=(
-            jax.ShapeDtypeStruct((planes, double, share * LANES), f32),
+            jax.ShapeDtypeStruct((planes, tile, share * LANES), f32),
             jax.ShapeDtypeStruct((rows, side), f32),
         ),
-        in_specs=[hbm, hbm, hbm],
+        in_specs=[hbm, hbm],
         out_specs=(vmem, vmem),
         scratch_shapes=scratch,
         compiler_params=pltpu.CompilerParams(
-            vmem_limit_bytes=VMEM_LIMIT, collective_id=0, has_side_effects=True
+            vmem_limit_bytes=EXCHANGE_VMEM, collective_id=0, has_side_effects=True
         ),
         name="exchange",
-    )(grad_a, grad_b, prb.reshape(rows, side))
+    )(grad, prb.reshape(rows, side))
 
 
 def wave_sum(block):
@@ -413,22 +397,122 @@
     return total.transpose(1, 2, 0, 3).reshape(2, block.shape[2], share * LANES)
 
 
+def rim_kernel(regions, field, rim, sems):
+    side = rim.shape[1]
+    me, wave = lax.axis_index("region"), lax.axis_index("wave")
+    first, last = me == 0, me == regions - 1
+    odd = lax.rem(me, 2) == 1
+    behind, ahead = lax.rem(me + regions - 1, regions), lax.rem(me + 1, regions)
+    part = side // PIECES
+
+    @pl.when(last)
+    def _():
+        rim[...] = jnp.zeros_like(rim)
+
+    barrier = pltpu.get_barrier_semaphore()
+    for target in ({"wave": 1 - wave}, {"region": behind}, {"region": ahead}):
+        pl.semaphore_signal(
+            barrier, inc=1, device_id=target, device_id_type=pl.DeviceIdType.MESH
+        )
+    pl.semaphore_wait(barrier, 3)
+
+    def remote(src, dst, row, index, target):
+        return pltpu.make_async_remote_copy(
+            src_ref=src,
+            dst_ref=dst,
+            send_sem=sems.at[row, index],
+            recv_sem=sems.at[row + 1, index],
+            device_id=target,
+            device_id_type=pl.DeviceIdType.MESH,
+        )
+
+    whole = remote(field.at[:, pl.ds(0, side)], rim, 0, PIECES, {"region": behind})
+    pieces = [
+        remote(
+            field.at[wave, pl.ds(j * part, part)],
+            rim.at[wave, pl.ds(j * part, part)],
+            0,
+            j,
+            {"region": behind},
+        )
+        for j in range(PIECES)
+    ]
+    relays = [
+        remote(
+            rim.at[wave, pl.ds(j * part, part)],
+            rim.at[wave, pl.ds(j * part, part)],
+            2,
+            j,
+            {"wave": 1 - wave},
+        )
+        for j in range(PIECES)
+    ]
+    sends_pieces = jnp.logical_not(odd) & jnp.logical_not(first)
+    relaying = odd & jnp.logical_not(last)
+
+    @pl.when(odd)
+    def _():
+        whole.start()
+
+    @pl.when(sends_pieces)
+    def _():
+        for piece in pieces:
+            piece.start()
+
+    @pl.when(relaying)
+    def _():
+        for piece, relay in zip(pieces, relays):
+            piece.wait_recv()
+            relay.start()
+        for relay in relays:
+            relay.wait()
+
+    @pl.when(jnp.logical_not(odd))
+    def _():
+        whole.wait_recv()
+
+    @pl.when(odd)
+    def _():
+        whole.wait_send()
+
+    @pl.when(sends_pieces)
+    def _():
+        for piece in pieces:
+            piece.wait_send()
+
+
+def rim_call(field, side, regions):
+    return pl.pallas_call(
+        functools.partial(rim_kernel, regions),
+        out_shape=jax.ShapeDtypeStruct((field.shape[0], side, field.shape[2]), jnp.float32),
+        in_specs=[pl.BlockSpec(memory_space=pl.ANY)],
+        out_specs=pl.BlockSpec(memory_space=pltpu.VMEM),
+        scratch_shapes=[pltpu.SemaphoreType.DMA((4, PIECES + 1))],
+        compiler_params=pltpu.CompilerParams(
+            vmem_limit_bytes=RIM_VMEM, collective_id=1, has_side_effects=True
+        ),
+        name="rim",
+    )(field)
+
+
 def on_device(object_field, probes, patterns, offsets, counts):
     side = probes.shape[-1]
+    tile = object_field.shape[1]
     waves, regions = lax.axis_size("wave"), lax.axis_size("region")
+    paired = waves == 2 and regions & (regions - 1) == 0
     tables = make_tables(side)
-    rim = from_behind(object_field[:, :side, :], "region", -1)
-    grad_a, prb_a = patch_call(False, offsets, counts, object_field, (), probes, patterns, tables)
-    grad_b, prb_b = patch_call(
-        True, offsets, counts, object_field, (rim, grad_a, prb_a), probes, patterns, tables
-    )
-    if waves == 2 and regions & (regions - 1) == 0:
-        object_out, probe_total = exchange_call(grad_a, grad_b, prb_b, waves, regions)
-        return (object_out, probe_total.reshape((1,) + prb_b.shape))
-    arrived = from_behind(grad_b[:, :, side:, :], "region", 1)
-    probe_total = lax.psum(prb_b, "region")
-    bottom = wave_sum(grad_b[:, :, :side, :])
-    top = wave_sum(grad_a[:, :, :side, :] + arrived)
+    if paired:
+        rim = rim_call(object_field, side, regions)
+    else:
+        rim = from_behind(object_field[:, :side, :], "region", -1)
+    grad, prb = patch_call(offsets, counts, object_field, rim, probes, patterns, tables)
+    if paired:
+        object_out, probe_total = exchange_call(grad, prb, waves, regions)
+        return (object_out, probe_total.reshape((1,) + prb.shape))
+    arrived = from_behind(grad[:, :, tile:, :], "region", 1)
+    probe_total = lax.psum(prb, "region")
+    bottom = wave_sum(grad[:, :, side:tile, :])
+    top = wave_sum(grad[:, :, :side, :] + arrived)
     return (jnp.concatenate([top, bottom], axis=1), probe_total[None])
 
 

time: 114 us -> 110 us (0.965); the launches traced: 115 us -> 110 us
  Pallas kernels: 106 us -> 100 us
  local copies, waits for them, and re-layouts: 6.34 us -> 8.18 us
  starting transfers between devices: 1.29 us -> 0 us
    pallas_call x3, Pallas kernels: 106 us -> 100 us  [the longest x1 81.3 us: exchange_call(): pl.pallas_call(functools.partial(exchange_kernel, regions), out_shape=(ja...]
    unnamed x7 -> x15, local copies, waits for them, and re-layouts: 4.61 us -> 8.18 us
    slice x1 -> x0, local copies, waits for them, and re-layouts: 1.73 us -> none  [on_device(): rim = from_behind(object_field[:, :side, :], 'region', -1)]
    ppermute x1 -> x0, starting transfers between devices: 1.29 us -> none  [from_behind(): return lax.ppermute(block, axis, route)]
  transfers between devices with their start and end apart: 1 -> 0, of which waited for: 0 -> 0; matrix products, arithmetic and copies ran while one was open for 1% -> 0% of each run, Pallas kernels for 10% -> 0%
where the time goes in v3:
time: 110 us
  Pallas kernels  100 us (91%)
  local copies, waits for them, and re-layouts  8.18 us (7%)
  between operations  1.33 us (1%)
    pallas_call x1, Pallas kernels, exchange_call(): pl.pallas_call(functools.partial(exchange_kernel, regions), out_shape=(ja...  81.3 us
    pallas_call x1, Pallas kernels, patch_call(): pl.pallas_call(functools.partial(patch_kernel, side, tile, slots, width),...  12.1 us
    unnamed x15, local copies, waits for them, and re-layouts  8.18 us
    pallas_call x1, Pallas kernels, rim_call(): pl.pallas_call(functools.partial(rim_kernel, regions), out_shape=jax.Shap...  6.91 us

profile of v3, /device:TPU:0, one launch (start us, length us, event | category | flops | bytes accessed | tf_op | source)
XLA Modules:
  0.0 109.8 jit_solution(11354021190415939321)
XLA Ops:
  1.3 0.8 copy.9.refs_0_
  2.0 0.0 copy-start
  2.0 2.2 %copy-done = f32[2,512,1024]{2,1,0:T(8,128)S(1)} copy-done((f32[2,512,1024]{2,1,0:T(8,128)S(1)}, f32[2,512,1024]{2,1,0:T(8,128)}, u32[]{:S(2)}) %copy-start) | copy-done | bytes 4194328
  4.2 0.0 copy-start.1
  4.2 0.0 copy-start.2
  4.2 6.9 %rim.1.refs_3_ = f32[2,256,1024]{2,1,0:T(8,128)S(1)} custom-call(f32[2,512,1024]{2,1,0:T(8,128)S(1)} %copy-done), custom_call_target="tpu_custom_call" | custom-call | tf_op jit(solution)/shard_map/rim/pallas_call | solution.py:485
  11.1 0.0 copy-done.1
  11.2 0.0 copy-done.2
  11.2 0.0 copy-start.3
  11.2 1.0 copy-done.3
  12.2 0.0 copy-start.4
  12.2 1.0 copy-done.4
  13.3 0.0 copy-start.5
  13.3 1.0 copy-done.5
  14.3 12.1 %patches.1 = (f32[8,2,768,128]{3,2,1,0:T(8,128)S(1)}, f32[2,256,256]{2,1,0:T(8,128)S(1)}) custom-call(s32[16,2]{1,0:T(8,128)S(1)} %copy.9.refs_0_, s32[1]{0:T(128)S(6)} %copy.12.refs_1_, f32[2,512,1024]{2,1,0:T(8,128)S(1)} %copy-done.1, f32[2,256,1024]{2,1,0:T(8,128)S(1)} %rim.1.refs_3_, f32[1,2,256,256]{3,2,1,0:T(8,128)S(1)} %copy-done.3, ...), custom_call_target="tpu_custom_call" | custom-call | flops 4294967296 | bytes 20971520 | tf_op jit(solution)/shard_map/patches/pallas_call | solution.py:188
  26.4 81.3 %exchange.1 = (f32[2,512,512]{2,1,0:T(8,128)S(1)}, f32[512,256]{1,0:T(8,128)S(1)}) custom-call(f32[8,2,768,128]{3,2,1,0:T(8,128)S(1)} %get-tuple-element.6.grad_ref, f32[512,256]{1,0:T(8,128)S(1)} %bitcast.3), custom_call_target="tpu_custom_call" | custom-call | tf_op jit(solution)/shard_map/exchange/pallas_call | solution.py:378
  107.7 1.3 %copy.13 = f32[2,512,512]{2,1,0:T(8,128)} copy(f32[2,512,512]{2,1,0:T(8,128)S(1)} %get-tuple-element.12) | data formatting | bytes 4194304
  109.1 0.8 copy.14
Async XLA Ops:
  2.0 2.2 %copy-start = (f32[2,512,1024]{2,1,0:T(8,128)S(1)}, f32[2,512,1024]{2,1,0:T(8,128)}, u32[]{:S(2)}) copy-start(f32[2,512,1024]{2,1,0:T(8,128)} %refs_2_.1) | copy-start | bytes 12582916
  4.2 6.9 %copy-start.1 = (f32[2,512,1024]{2,1,0:T(8,128)S(1)}, f32[2,512,1024]{2,1,0:T(8,128)}, u32[]{:S(2)}) copy-start(f32[2,512,1024]{2,1,0:T(8,128)} %refs_2_.1) | copy-start | bytes 12582916
  4.2 6.9 %copy-start.2 = (bf16[1,16,256,256]{3,2,1,0:T(8,128)(2,1)S(1)}, bf16[1,16,256,256]{3,2,1,0:T(8,128)(2,1)}, u32[]{:S(2)}) copy-start(bf16[1,16,256,256]{3,2,1,0:T(8,128)(2,1)} %refs_5_.1) | copy-start | bytes 6291460
  11.2 1.0 copy-start.3
  12.2 1.0 copy-start.4
  13.3 1.0 copy-start.5

commit v4 on v3

--- a/solution.py
+++ b/solution.py
@@ -15,7 +15,7 @@
 PATCH_VMEM = 28 * 1024 * 1024
 EXCHANGE_VMEM = 20 * 1024 * 1024
 RIM_VMEM = 8 * 1024 * 1024
-PIECES = 4
+PIECES = 8
 
 
 def from_behind(block, axis, distance):
@@ -287,11 +287,25 @@
 
     @pl.when(jnp.logical_not(last))
     def _():
-        for copy in halo_copies[1:]:
+        for copy in halo_copies[1:share]:
             copy.start()
 
     for copy in locals_:
         copy.wait()
+
+    tops = []
+    for j in range(share):
+        pl.when(jnp.logical_not(first))(lambda j=j: halo_copies[j].wait_recv())
+        top_out[j] = a_top[other + j] + halo[other + j]
+        copy = remote(
+            top_out.at[j], top_in.at[j], top_send.at[j], top_recv.at[j], "wave", 1 - wave
+        )
+        copy.start()
+        tops.append(copy)
+
+    @pl.when(jnp.logical_not(last))
+    def _():
+        halo_copies[share].start()
 
     start, size = jnp.int32(0), acc.shape[0]
     for bit in range(bits):
@@ -311,16 +325,6 @@
         copy.wait()
         acc[pl.ds(start, size), :] += stages[bit][...]
     full[pl.ds(start, size), :] = acc[pl.ds(start, size), :]
-
-    tops = []
-    for j in range(share):
-        pl.when(jnp.logical_not(first))(lambda j=j: halo_copies[j].wait_recv())
-        top_out[j] = a_top[other + j] + halo[other + j]
-        copy = remote(
-            top_out.at[j], top_in.at[j], top_send.at[j], top_recv.at[j], "wave", 1 - wave
-        )
-        copy.start()
-        tops.append(copy)
 
     for bit in reversed(range(bits)):
         value, target = flipped(bit)
@@ -456,7 +460,9 @@
 
     @pl.when(sends_pieces)
     def _():
-        for piece in pieces:
+        for j, piece in enumerate(pieces):
+            if j >= 2:
+                pieces[j - 2].wait_send()
             piece.start()
 
     @pl.when(relaying)
@@ -477,7 +483,7 @@
 
     @pl.when(sends_pieces)
     def _():
-        for piece in pieces:
+        for piece in pieces[-2:]:
             piece.wait_send()
 
 

time: 110 us -> 98 us (0.89)
  Pallas kernels: 100 us -> 88.2 us
    pallas_call x1, Pallas kernels: 81.3 us -> 64.3 us  [exchange_call(): pl.pallas_call(functools.partial(exchange_kernel, regions), out_shape=(ja...]
    pallas_call x1, Pallas kernels: 12.1 us -> 16.8 us  [patch_call(): pl.pallas_call(functools.partial(patch_kernel, side, tile, slots, width),...]
where the time goes in v4:
time: 98 us; the launch traced here: 97.7 us
  Pallas kernels  88.2 us (90%)
  local copies, waits for them, and re-layouts  8.18 us (8%)
  between operations  1.33 us (1%)
    pallas_call x1, Pallas kernels, exchange_call(): pl.pallas_call(functools.partial(exchange_kernel, regions), out_shape=(ja...  64.3 us
    pallas_call x1, Pallas kernels, patch_call(): pl.pallas_call(functools.partial(patch_kernel, side, tile, slots, width),...  16.8 us
    unnamed x15, local copies, waits for them, and re-layouts  8.18 us
    pallas_call x1, Pallas kernels, rim_call(): pl.pallas_call(functools.partial(rim_kernel, regions), out_shape=jax.Shap...  7.05 us

profile of v4, /device:TPU:0, one launch (start us, length us, event | category | flops | bytes accessed | tf_op | source)
XLA Modules:
  0.0 97.7 jit_solution(6149455170942072129)
XLA Ops:
  1.3 0.8 copy.9.refs_0_
  2.0 0.0 copy-start
  2.0 2.2 %copy-done = f32[2,512,1024]{2,1,0:T(8,128)S(1)} copy-done((f32[2,512,1024]{2,1,0:T(8,128)S(1)}, f32[2,512,1024]{2,1,0:T(8,128)}, u32[]{:S(2)}) %copy-start) | copy-done | bytes 4194328
  4.2 0.0 copy-start.1
  4.2 0.0 copy-start.2
  4.2 7.1 %rim.1.refs_3_ = f32[2,256,1024]{2,1,0:T(8,128)S(1)} custom-call(f32[2,512,1024]{2,1,0:T(8,128)S(1)} %copy-done), custom_call_target="tpu_custom_call" | custom-call | tf_op jit(solution)/shard_map/rim/pallas_call | solution.py:491
  11.3 0.0 copy-done.1
  11.3 0.0 copy-done.2
  11.3 0.0 copy-start.3
  11.3 1.0 %copy-done.3 = f32[1,2,256,256]{3,2,1,0:T(8,128)S(1)} copy-done((f32[1,2,256,256]{3,2,1,0:T(8,128)S(1)}, f32[1,2,256,256]{3,2,1,0:T(8,128)}, u32[]{:S(2)}) %copy-start.3) | copy-done | bytes 524312
  12.4 0.0 copy-start.4
  12.4 1.0 %copy-done.4 = bf16[512,512]{1,0:T(8,128)(2,1)S(1)} copy-done((bf16[512,512]{1,0:T(8,128)(2,1)S(1)}, bf16[512,512]{1,0:T(8,128)(2,1)}, u32[]{:S(2)}) %copy-start.4) | copy-done | bytes 524312
  13.4 0.0 copy-start.5
  13.4 1.0 %copy-done.5 = bf16[512,512]{1,0:T(8,128)(2,1)S(1)} copy-done((bf16[512,512]{1,0:T(8,128)(2,1)S(1)}, bf16[512,512]{1,0:T(8,128)(2,1)}, u32[]{:S(2)}) %copy-start.5) | copy-done | bytes 524312
  14.4 16.8 %patches.1 = (f32[8,2,768,128]{3,2,1,0:T(8,128)S(1)}, f32[2,256,256]{2,1,0:T(8,128)S(1)}) custom-call(s32[16,2]{1,0:T(8,128)S(1)} %copy.9.refs_0_, s32[1]{0:T(128)S(6)} %copy.12.refs_1_, f32[2,512,1024]{2,1,0:T(8,128)S(1)} %copy-done.1, f32[2,256,1024]{2,1,0:T(8,128)S(1)} %rim.1.refs_3_, f32[1,2,256,256]{3,2,1,0:T(8,128)S(1)} %copy-done.3, ...), custom_call_target="tpu_custom_call" | custom-call | flops 4294967296 | bytes 20971520 | tf_op jit(solution)/shard_map/patches/pallas_call | solution.py:188
  31.3 64.3 %exchange.1 = (f32[2,512,512]{2,1,0:T(8,128)S(1)}, f32[512,256]{1,0:T(8,128)S(1)}) custom-call(f32[8,2,768,128]{3,2,1,0:T(8,128)S(1)} %get-tuple-element.6.grad_ref, f32[512,256]{1,0:T(8,128)S(1)} %bitcast.3), custom_call_target="tpu_custom_call" | custom-call | tf_op jit(solution)/shard_map/exchange/pallas_call | solution.py:382
  95.6 1.3 %copy.13 = f32[2,512,512]{2,1,0:T(8,128)} copy(f32[2,512,512]{2,1,0:T(8,128)S(1)} %get-tuple-element.12) | data formatting | bytes 4194304
  96.9 0.8 copy.14
Async XLA Ops:
  2.0 2.2 %copy-start = (f32[2,512,1024]{2,1,0:T(8,128)S(1)}, f32[2,512,1024]{2,1,0:T(8,128)}, u32[]{:S(2)}) copy-start(f32[2,512,1024]{2,1,0:T(8,128)} %refs_2_.1) | copy-start | bytes 12582916
  4.2 7.1 %copy-start.1 = (f32[2,512,1024]{2,1,0:T(8,128)S(1)}, f32[2,512,1024]{2,1,0:T(8,128)}, u32[]{:S(2)}) copy-start(f32[2,512,1024]{2,1,0:T(8,128)} %refs_2_.1) | copy-start | bytes 12582916
  4.2 7.1 %copy-start.2 = (bf16[1,16,256,256]{3,2,1,0:T(8,128)(2,1)S(1)}, bf16[1,16,256,256]{3,2,1,0:T(8,128)(2,1)}, u32[]{:S(2)}) copy-start(bf16[1,16,256,256]{3,2,1,0:T(8,128)(2,1)} %refs_5_.1) | copy-start | bytes 6291460
  11.3 1.0 %copy-start.3 = (f32[1,2,256,256]{3,2,1,0:T(8,128)S(1)}, f32[1,2,256,256]{3,2,1,0:T(8,128)}, u32[]{:S(2)}) copy-start(f32[1,2,256,256]{3,2,1,0:T(8,128)} %refs_4_.1) | copy-start | bytes 1572868
  12.4 1.0 %copy-start.4 = (bf16[512,512]{1,0:T(8,128)(2,1)S(1)}, bf16[512,512]{1,0:T(8,128)(2,1)}, u32[]{:S(2)}) copy-start(bf16[512,512]{1,0:T(8,128)(2,1)} %constant.5.clone.refs_7_) | copy-start | bytes 1572868
  13.4 1.0 %copy-start.5 = (bf16[512,512]{1,0:T(8,128)(2,1)S(1)}, bf16[512,512]{1,0:T(8,128)(2,1)}, u32[]{:S(2)}) copy-start(bf16[512,512]{1,0:T(8,128)(2,1)} %constant.4.clone.refs_6_) | copy-start | bytes 1572868
